TPU v7x, 32 devices: a whole 2x2x4 slice. The times are simulated.
32 devices in a mesh: rep: 4 (over z), fsdp: 8 (over y, x, core).
Axes of the slice: x: 2, y: 2, z: 4, core: 2. Of those that a mesh axis runs over, the one named last changes fastest.
Arguments:
- word_rows: bfloat16 [4096, 768], P(('rep', 'fsdp')), may hold values from -6 to 6
- region_rows: bfloat16 [8192, 768], P(('rep', 'fsdp')), may hold values from -6 to 6
- word_segment: int32 [32, 128], P(('rep', 'fsdp')), may hold values from 0 to 7, never falling along the last dimension, each value on 1 to 20 neighbouring positions
- region_segment: int32 [32, 256], P(('rep', 'fsdp')), may hold values from 0 to 7, never falling along the last dimension, each value on 1 to 36 neighbouring positions
- inward: bfloat16 [3, 768, 2304], P(None, 'fsdp'), may hold values from -0.21875 to 0.21875
- outward: bfloat16 [3, 768, 768], P(None, 'fsdp'), may hold values from -0.875 to 0.875
- biases: bfloat16 [16, 768], P(None, 'fsdp'), may hold values from -3 to 3
- norm_gain: bfloat16 [5, 768], P(None, 'fsdp'), may hold values from 0.5 to 1.5
- expand_weight: bfloat16 [2, 768, 3072], P(None, 'fsdp'), may hold values from -0.21875 to 0.21875
- shrink_weight: bfloat16 [2, 3072, 768], P(None, 'fsdp'), may hold values from -0.109375 to 0.109375
- hidden_bias: bfloat16 [2, 3072], P(None, 'fsdp'), may hold values from -3 to 3
- word_cotangent: bfloat16 [4096, 768], P(('rep', 'fsdp')), may hold values from -6 to 6
- region_cotangent: bfloat16 [8192, 768], P(('rep', 'fsdp')), may hold values from -6 to 6
Outputs:
- word_output: bfloat16 [4096, 768], P(('rep', 'fsdp'))
- region_output: bfloat16 [8192, 768], P(('rep', 'fsdp'))
- word_gradient: float32 [4096, 768], P(('rep', 'fsdp'))
- region_gradient: float32 [8192, 768], P(('rep', 'fsdp'))
- inward_grad: float32 [3, 768, 2304], P(None, 'fsdp')
- outward_grad: float32 [3, 768, 768], P(None, 'fsdp')
- biases_grad: float32 [16, 768], P(None, 'fsdp')
- gain_grad: float32 [5, 768], P(None, 'fsdp')
- expand_grad: float32 [2, 768, 3072], P(None, 'fsdp')
- shrink_grad: float32 [2, 3072, 768], P(None, 'fsdp')
- hidden_grad: float32 [2, 3072], P(None, 'fsdp')
Inputs may be any that keep to these rules, and one draw needn't show every extreme that they name: Row g of word_segment gives the ids of the g-th block of 128 word rows: they never fall, every id from 0 to 7 occurs, and an id covers 1 to 20 positions. Equal ids in the same row of word_segment and region_segment name one caption-region pair. Row g of region_segment gives the ids of the g-th block of 256 region rows: they never fall, every id from 0 to 7 occurs, and an id covers 1 to 36 positions.
All inputs are finite; a program needn't handle non-finite values.
Results may differ from a plain program's by a relative error of at most 0.018.
Values may be sent and summed in bfloat16 or wider, within the bound.
A program may use at most 256 MiB of HBM per device.

v0:
```python
import jax
import jax.numpy as jnp
from jax import lax
from jax.sharding import PartitionSpec as P

HEADS = 12
HEAD_DIM = 64


norm_epsilon = 1e-12
masked_score = -1e30


def matmul(left_op, right_op):
    return jnp.dot(left_op, right_op, preferred_element_type=jnp.float32)


def matmul_tn(left_op, right_op):
    return lax.dot_general(
        left_op, right_op, (((0,), (0,)), ((), ())), preferred_element_type=jnp.float32
    )


def matmul_nt(left_op, right_op):
    return lax.dot_general(
        left_op, right_op, (((1,), (1,)), ((), ())), preferred_element_type=jnp.float32
    )


def column_sums(values):
    return jnp.sum(values, axis=0, dtype=jnp.float32)


def heads_of(rows_in):
    return rows_in.reshape(rows_in.shape[0], HEADS, HEAD_DIM)


def merge_heads(head_rows):
    return head_rows.reshape(head_rows.shape[0], -1)


def normalize(summed, gain_row, shift_row):
    center = summed - jnp.mean(summed, axis=-1, keepdims=True)
    inverse = lax.rsqrt(jnp.mean(center * center, axis=-1, keepdims=True) + norm_epsilon)
    normed = center * inverse
    return (normed * gain_row + shift_row, (normed, inverse))


def normalize_back(grad_out, norm_stats, gain_row):
    normed, inverse = norm_stats
    grad_normed = grad_out * gain_row
    grad_sum = inverse * (
        grad_normed
        - jnp.mean(grad_normed, axis=-1, keepdims=True)
        - normed * jnp.mean(grad_normed * normed, axis=-1, keepdims=True)
    )
    return (grad_sum, column_sums(grad_out * normed), column_sums(grad_out))


def score_block(queries, key_rows, allowed):
    scores = jnp.einsum(
        "qhd,khd->hqk", heads_of(queries), heads_of(key_rows), preferred_element_type=jnp.float32
    ) * HEAD_DIM ** (-0.5)
    return jnp.where(allowed[None], scores, masked_score)


def attend(queries, key_rows, value_rows, allowed):
    scores = score_block(queries, key_rows, allowed)
    top_score = jnp.max(scores, axis=-1, keepdims=True)
    log_total = top_score + jnp.log(jnp.sum(jnp.exp(scores - top_score), axis=-1, keepdims=True))
    shares = jnp.exp(scores - log_total).astype(jnp.bfloat16)
    context = jnp.einsum(
        "hqk,khd->qhd", shares, heads_of(value_rows), preferred_element_type=jnp.float32
    )
    return (merge_heads(context).astype(jnp.bfloat16), log_total)


def attend_back(queries, key_rows, value_rows, allowed, log_total, grad_context):
    shares = jnp.exp(score_block(queries, key_rows, allowed) - log_total)
    grad_heads = heads_of(grad_context)
    grad_shares = jnp.einsum(
        "qhd,khd->hqk", grad_heads, heads_of(value_rows), preferred_element_type=jnp.float32
    )
    grad_values = jnp.einsum(
        "hqk,qhd->khd", shares.astype(jnp.bfloat16), grad_heads, preferred_element_type=jnp.float32
    )
    grad_scores = (
        shares * (grad_shares - jnp.sum(shares * grad_shares, axis=-1, keepdims=True))
    ).astype(jnp.bfloat16)
    score_scale = HEAD_DIM ** (-0.5)
    grad_queries = (
        jnp.einsum(
            "hqk,khd->qhd", grad_scores, heads_of(key_rows), preferred_element_type=jnp.float32
        )
        * score_scale
    )
    grad_keys = (
        jnp.einsum(
            "hqk,qhd->khd", grad_scores, heads_of(queries), preferred_element_type=jnp.float32
        )
        * score_scale
    )
    return (merge_heads(grad_queries), merge_heads(grad_keys), merge_heads(grad_values))


def project(rows_low, weight, bias_rows, module):
    width = weight.shape[0]
    bias_all = jnp.concatenate(
        [bias_rows[3 * module], jnp.zeros((width,), jnp.float32), bias_rows[3 * module + 1]]
    )
    return (matmul(rows_low, weight) + bias_all).astype(jnp.bfloat16)


def project_back(grad_sum, grad_parts, rows_low, weight):
    width = weight.shape[0]
    grad_mixed = jnp.concatenate(grad_parts, axis=1).astype(jnp.bfloat16)
    grad_weight = matmul_tn(rows_low, grad_mixed)
    grad_bias = column_sums(grad_mixed)
    grad_rows = grad_sum + matmul_nt(grad_mixed, weight)
    return (grad_rows, grad_weight, grad_bias[:width], grad_bias[2 * width :])


def branch_back(grad_out, context, norm_stats, gain_row, outward_one):
    grad_sum, grad_gain, grad_shift = normalize_back(grad_out, norm_stats, gain_row)
    grad_branch = grad_sum.astype(jnp.bfloat16)
    grad_outward = matmul_tn(context, grad_branch)
    grad_context = matmul_nt(grad_branch, outward_one).astype(jnp.bfloat16)
    return (grad_sum, grad_context, grad_outward, column_sums(grad_branch), grad_gain, grad_shift)


def self_forward(rows_in, weights, module, allowed):
    inward_all, outward_all, bias_rows, gain_rows = weights
    width = rows_in.shape[1]
    rows_low = rows_in.astype(jnp.bfloat16)
    mixed = project(rows_low, inward_all[module], bias_rows, module)
    context, log_total = attend(
        mixed[:, :width], mixed[:, width : 2 * width], mixed[:, 2 * width :], allowed
    )
    summed = rows_in + matmul(context, outward_all[module]) + bias_rows[3 * module + 2]
    result, norm_stats = normalize(summed, gain_rows[module], bias_rows[9 + module])
    return (result, (rows_low, mixed, context, log_total, norm_stats))


def self_backward(grad_out, kept, weights, module, allowed):
    inward_all, outward_all, bias_rows, gain_rows = weights
    rows_low, mixed, context, log_total, norm_stats = kept
    width = rows_low.shape[1]
    grad_sum, grad_context, grad_outward, grad_bias_out, grad_gain, grad_shift = branch_back(
        grad_out, context, norm_stats, gain_rows[module], outward_all[module]
    )
    grad_parts = attend_back(
        mixed[:, :width],
        mixed[:, width : 2 * width],
        mixed[:, 2 * width :],
        allowed,
        log_total,
        grad_context,
    )
    grad_rows, grad_inward, grad_bias_query, grad_bias_value = project_back(
        grad_sum, grad_parts, rows_low, inward_all[module]
    )
    return (
        grad_rows,
        grad_inward,
        grad_outward,
        (grad_bias_query, grad_bias_value, grad_bias_out),
        grad_gain,
        grad_shift,
    )


def cross_forward(word_rows, region_rows, weights, cross_mask):
    inward_all, outward_all, bias_rows, gain_rows = weights
    words_count = word_rows.shape[0]
    width = word_rows.shape[1]
    rows_low = jnp.concatenate([word_rows, region_rows], axis=0)
    mixed = project(rows_low, inward_all[0], bias_rows, 0)
    word_mix = mixed[:words_count]
    region_mix = mixed[words_count:]
    word_context, word_total = attend(
        word_mix[:, :width],
        region_mix[:, width : 2 * width],
        region_mix[:, 2 * width :],
        cross_mask,
    )
    region_context, region_total = attend(
        region_mix[:, :width],
        word_mix[:, width : 2 * width],
        word_mix[:, 2 * width :],
        cross_mask.T,
    )
    context = jnp.concatenate([word_context, region_context], axis=0)
    summed = rows_low.astype(jnp.float32) + matmul(context, outward_all[0]) + bias_rows[2]
    result, norm_stats = normalize(summed, gain_rows[0], bias_rows[9])
    return (result, (rows_low, mixed, context, word_total, region_total, norm_stats))


def cross_backward(grad_out, kept, weights, cross_mask, words_count):
    inward_all, outward_all, bias_rows, gain_rows = weights
    rows_low, mixed, context, word_total, region_total, norm_stats = kept
    width = rows_low.shape[1]
    grad_sum, grad_context, grad_outward, grad_bias_out, grad_gain, grad_shift = branch_back(
        grad_out, context, norm_stats, gain_rows[0], outward_all[0]
    )
    word_mix = mixed[:words_count]
    region_mix = mixed[words_count:]
    word_query_grad, region_key_grad, region_value_grad = attend_back(
        word_mix[:, :width],
        region_mix[:, width : 2 * width],
        region_mix[:, 2 * width :],
        cross_mask,
        word_total,
        grad_context[:words_count],
    )
    region_query_grad, word_key_grad, word_value_grad = attend_back(
        region_mix[:, :width],
        word_mix[:, width : 2 * width],
        word_mix[:, 2 * width :],
        cross_mask.T,
        region_total,
        grad_context[words_count:],
    )
    grad_parts = (
        jnp.concatenate([word_query_grad, region_query_grad], axis=0),
        jnp.concatenate([word_key_grad, region_key_grad], axis=0),
        jnp.concatenate([word_value_grad, region_value_grad], axis=0),
    )
    grad_rows, grad_inward, grad_bias_query, grad_bias_value = project_back(
        grad_sum, grad_parts, rows_low, inward_all[0]
    )
    return (
        grad_rows,
        grad_inward,
        grad_outward,
        (grad_bias_query, grad_bias_value, grad_bias_out),
        grad_gain,
        grad_shift,
    )


def gelu_exact(values):
    return jax.nn.gelu(values, approximate=False)


def feed_forward(rows_in, weights, feed_index, attend_set):
    expand_all, shrink_all, hidden_all = weights
    bias_rows, gain_rows = (attend_set[2], attend_set[3])
    rows_low = rows_in.astype(jnp.bfloat16)
    before = matmul(rows_low, expand_all[feed_index]) + hidden_all[feed_index].astype(jnp.float32)
    hidden = gelu_exact(before).astype(jnp.bfloat16)
    summed = rows_in + matmul(hidden, shrink_all[feed_index]) + bias_rows[14 + feed_index]
    result, norm_stats = normalize(summed, gain_rows[3 + feed_index], bias_rows[12 + feed_index])
    return (result, (rows_low, before, hidden, norm_stats))


def feed_backward(grad_out, kept, weights, feed_index, gain_rows):
    expand_all, shrink_all, hidden_all = weights
    rows_low, before, hidden, norm_stats = kept
    grad_sum, grad_gain, grad_shift = normalize_back(
        grad_out, norm_stats, gain_rows[3 + feed_index]
    )
    grad_branch = grad_sum.astype(jnp.bfloat16)
    grad_shrink = matmul_tn(hidden, grad_branch)
    grad_hidden = matmul_nt(grad_branch, shrink_all[feed_index])
    unused_value, slope_back = jax.vjp(gelu_exact, before)
    grad_before = slope_back(grad_hidden)[0].astype(jnp.bfloat16)
    grad_expand = matmul_tn(rows_low, grad_before)
    grad_rows = grad_sum + matmul_nt(grad_before, expand_all[feed_index])
    return (
        grad_rows,
        grad_expand,
        grad_shrink,
        column_sums(grad_before),
        column_sums(grad_branch),
        grad_gain,
        grad_shift,
    )


def local(
    word_rows,
    region_rows,
    word_segment,
    region_segment,
    inward,
    outward,
    biases,
    norm_gain,
    expand_weight,
    shrink_weight,
    hidden_bias,
    word_cotangent,
    region_cotangent,
):
    words_count = word_rows.shape[0]
    word_ids = word_segment[0]
    region_ids = region_segment[0]
    cross_mask = word_ids[:, None] == region_ids[None, :]
    word_mask = word_ids[:, None] == word_ids[None, :]
    region_mask = region_ids[:, None] == region_ids[None, :]
    inward_all, outward_all, bias_all, gain_all = (
        lax.all_gather(inward, "fsdp", axis=1, tiled=True),
        lax.all_gather(outward, "fsdp", axis=1, tiled=True),
        lax.all_gather(biases, "fsdp", axis=1, tiled=True),
        lax.all_gather(norm_gain, "fsdp", axis=1, tiled=True),
    )
    attend_set = (
        inward_all,
        outward_all,
        bias_all.astype(jnp.float32),
        gain_all.astype(jnp.float32),
    )
    crossed, unused_kept = cross_forward(word_rows, region_rows, attend_set, cross_mask)
    word_one, word_kept = self_forward(crossed[:words_count], attend_set, 1, word_mask)
    region_one, region_kept = self_forward(crossed[words_count:], attend_set, 2, region_mask)
    expand_all, shrink_all, hidden_all = (
        lax.all_gather(expand_weight, "fsdp", axis=1, tiled=True),
        lax.all_gather(shrink_weight, "fsdp", axis=1, tiled=True),
        lax.all_gather(hidden_bias, "fsdp", axis=1, tiled=True),
    )
    feed_set = (expand_all, shrink_all, hidden_all)
    word_two, word_feed = feed_forward(word_one, feed_set, 0, attend_set)
    region_two, region_feed = feed_forward(region_one, feed_set, 1, attend_set)
    expand_again, shrink_again, hidden_again = (
        lax.all_gather(expand_weight, "fsdp", axis=1, tiled=True),
        lax.all_gather(shrink_weight, "fsdp", axis=1, tiled=True),
        lax.all_gather(hidden_bias, "fsdp", axis=1, tiled=True),
    )
    feed_later = (expand_again, shrink_again, hidden_again)
    word_back = feed_backward(
        word_cotangent.astype(jnp.float32), word_feed, feed_later, 0, attend_set[3]
    )
    region_back = feed_backward(
        region_cotangent.astype(jnp.float32), region_feed, feed_later, 1, attend_set[3]
    )
    expand_grad = jnp.stack([word_back[1], region_back[1]])
    shrink_grad = jnp.stack([word_back[2], region_back[2]])
    hidden_grad = jnp.stack([word_back[3], region_back[3]])
    inward_again, outward_again, bias_again, gain_again = (
        lax.all_gather(inward, "fsdp", axis=1, tiled=True),
        lax.all_gather(outward, "fsdp", axis=1, tiled=True),
        lax.all_gather(biases, "fsdp", axis=1, tiled=True),
        lax.all_gather(norm_gain, "fsdp", axis=1, tiled=True),
    )
    attend_later = (
        inward_again,
        outward_again,
        bias_again.astype(jnp.float32),
        gain_again.astype(jnp.float32),
    )
    word_self = self_backward(word_back[0], word_kept, attend_later, 1, word_mask)
    region_self = self_backward(region_back[0], region_kept, attend_later, 2, region_mask)
    again_words, again_regions = lax.optimization_barrier((word_rows, region_rows))
    unused_rows, cross_kept = cross_forward(again_words, again_regions, attend_later, cross_mask)
    grad_crossed = jnp.concatenate([word_self[0], region_self[0]], axis=0)
    cross_back = cross_backward(grad_crossed, cross_kept, attend_later, cross_mask, words_count)
    inward_grad = jnp.stack([cross_back[1], word_self[1], region_self[1]])
    outward_grad = jnp.stack([cross_back[2], word_self[2], region_self[2]])
    bias_grad = jnp.stack(
        [
            cross_back[3][0],
            cross_back[3][1],
            cross_back[3][2],
            word_self[3][0],
            word_self[3][1],
            word_self[3][2],
            region_self[3][0],
            region_self[3][1],
            region_self[3][2],
            cross_back[5],
            word_self[5],
            region_self[5],
            word_back[6],
            region_back[6],
            word_back[4],
            region_back[4],
        ]
    )
    gain_grad = jnp.stack(
        [cross_back[4], word_self[4], region_self[4], word_back[5], region_back[5]]
    )
    inward_part, outward_part, bias_part, gain_part, expand_part, shrink_part, hidden_part = (
        lax.psum_scatter(inward_grad, "fsdp", scatter_dimension=1, tiled=True),
        lax.psum_scatter(outward_grad, "fsdp", scatter_dimension=1, tiled=True),
        lax.psum_scatter(bias_grad, "fsdp", scatter_dimension=1, tiled=True),
        lax.psum_scatter(gain_grad, "fsdp", scatter_dimension=1, tiled=True),
        lax.psum_scatter(expand_grad, "fsdp", scatter_dimension=1, tiled=True),
        lax.psum_scatter(shrink_grad, "fsdp", scatter_dimension=1, tiled=True),
        lax.psum_scatter(hidden_grad, "fsdp", scatter_dimension=1, tiled=True),
    )
    summed_shares = (
        lax.psum_scatter(
            inward_part.astype(jnp.bfloat16), "rep", scatter_dimension=2, tiled=True
        ).astype(jnp.float32),
        lax.psum_scatter(
            outward_part.astype(jnp.bfloat16), "rep", scatter_dimension=2, tiled=True
        ).astype(jnp.float32),
        lax.psum_scatter(
            expand_part.astype(jnp.bfloat16), "rep", scatter_dimension=2, tiled=True
        ).astype(jnp.float32),
        lax.psum_scatter(
            shrink_part.astype(jnp.bfloat16), "rep", scatter_dimension=2, tiled=True
        ).astype(jnp.float32),
    )
    matrix_totals = (
        lax.all_gather(summed_shares[0].astype(jnp.bfloat16), "rep", axis=2, tiled=True).astype(
            jnp.float32
        ),
        lax.all_gather(summed_shares[1].astype(jnp.bfloat16), "rep", axis=2, tiled=True).astype(
            jnp.float32
        ),
        lax.all_gather(summed_shares[2].astype(jnp.bfloat16), "rep", axis=2, tiled=True).astype(
            jnp.float32
        ),
        lax.all_gather(summed_shares[3].astype(jnp.bfloat16), "rep", axis=2, tiled=True).astype(
            jnp.float32
        ),
    )
    small_totals = lax.psum((bias_part, gain_part, hidden_part), "rep")
    grad_rows = cross_back[0]
    return (
        word_two.astype(jnp.bfloat16),
        region_two.astype(jnp.bfloat16),
        grad_rows[:words_count],
        grad_rows[words_count:],
        matrix_totals[0],
        matrix_totals[1],
        small_totals[0],
        small_totals[1],
        matrix_totals[2],
        matrix_totals[3],
        small_totals[2],
    )


def solution(mesh):
    return jax.shard_map(
        local,
        mesh=mesh,
        in_specs=(
            P(("rep", "fsdp"), None),
            P(("rep", "fsdp"), None),
            P(("rep", "fsdp"), None),
            P(("rep", "fsdp"), None),
            P(None, "fsdp", None),
            P(None, "fsdp", None),
            P(None, "fsdp"),
            P(None, "fsdp"),
            P(None, "fsdp", None),
            P(None, "fsdp", None),
            P(None, "fsdp"),
            P(("rep", "fsdp"), None),
            P(("rep", "fsdp"), None),
        ),
        out_specs=(
            P(("rep", "fsdp"), None),
            P(("rep", "fsdp"), None),
            P(("rep", "fsdp"), None),
            P(("rep", "fsdp"), None),
            P(None, "fsdp", None),
            P(None, "fsdp", None),
            P(None, "fsdp"),
            P(None, "fsdp"),
            P(None, "fsdp", None),
            P(None, "fsdp", None),
            P(None, "fsdp"),
        ),
        check_vma=False,
    )
```

profile of v0, /device:TPU:0, one launch (start us, length us, event | category | flops | bytes accessed | tf_op | source)
XLA Modules:
  0.0 1144.1 jit_solution(15129114341354352432)
XLA Ops:
  10.1 10.5 all-gather
  20.7 8.9 all-gather.1
  29.7 7.9 all_gather.44
  40.2 36.4 %all-gather.10.cloned.1.call-done = bf16[3,768,2304]{2,1,0:T(8,128)(2,1)} async-done(((bf16[3,96,2304]{2,1,0:T(8,128)(2,1)}), bf16[3,768,2304]{2,1,0:T(8,128)(2,1)}) %all-gather.10.cloned.1.call-update) | async-done | bytes 10616848 | tf_op jit(solution)/shard_map/all_gather | solution.py:302
  87.3 25.2 %all-gather.12.cloned.1.call-done = bf16[3,768,768]{2,1,0:T(8,128)(2,1)} async-done(((bf16[3,96,768]{2,1,0:T(8,128)(2,1)}), bf16[3,768,768]{2,1,0:T(8,128)(2,1)}) %all-gather.12.cloned.1.call-update) | async-done | bytes 3538960 | tf_op jit(solution)/shard_map/all_gather | solution.py:303
  122.5 50.8 %all-gather.14.cloned.1.call-done = bf16[2,768,3072]{2,1,0:T(8,128)(2,1)} async-done(((bf16[2,96,3072]{2,1,0:T(8,128)(2,1)}), bf16[2,768,3072]{2,1,0:T(8,128)(2,1)}) %all-gather.14.cloned.1.call-update) | async-done | bytes 9437200 | tf_op jit(solution)/shard_map/all_gather | solution.py:317
  173.3 8.6 multiply_convert_fusion.4
  181.9 52.0 %all-gather.16.cloned.1.call-done = bf16[2,3072,768]{2,1,0:T(8,128)(2,1)} async-done(((bf16[2,384,768]{2,1,0:T(8,128)(2,1)}), bf16[2,3072,768]{2,1,0:T(8,128)(2,1)}) %all-gather.16.cloned.1.call-update) | async-done | bytes 9437200 | tf_op jit(solution)/shard_map/all_gather | solution.py:318
  249.1 11.5 %multiply_convert_fusion.1 = (bf16[256,3072]{1,0:T(8,128)(2,1)S(1)}, f32[256,3072]{1,0:T(8,128)}, f32[256,3072]{1,0:T(8,128)}) fusion(f32[3072]{0:T(1024)S(1)} %bitcast.383, bf16[2,768,3072]{2,1,0:T(8,128)(2,1)} %all-gather.14.cloned.1.call-done, f32[256,768]{1,0:T(8,128)S(1)} %get-tuple-element.141, f32[768]{0:T(1024)S(1)} %get-tuple-element.58, ...), kind=kOutput, calls=%fused_computation.43 | convolution fusion | flops 1260847104 | bytes 13389824 | tf_op jit(solution)/shard_map/dot_general | solution.py:15
  277.0 12.4 %reduce-scatter.25.cloned.1.call-start = ((), (), s32[]{:S(2)}) async-start(), calls=%async_computation.17 | async-start | bytes 21233664 | tf_op jit(solution)/shard_map/reduce_scatter | solution.py:387
  408.0 124.9 %reduce-scatter.25.cloned.1.call-done = f32[2,96,3072]{2,1,0:T(8,128)} async-done(((f32[2,768,3072]{2,1,0:T(8,128)}), f32[2,96,3072]{2,1,0:T(8,128)}) %reduce-scatter.25.cloned.1.call-update) | async-done | bytes 2359312 | tf_op jit(solution)/shard_map/reduce_scatter | solution.py:387
  535.8 137.9 %reduce-scatter.21.cloned.1.call-done = f32[3,96,2304]{2,1,0:T(8,128)} async-done(((f32[3,768,2304]{2,1,0:T(8,128)}), f32[3,96,2304]{2,1,0:T(8,128)}) %reduce-scatter.21.cloned.1.call-update) | async-done | bytes 2654224 | tf_op jit(solution)/shard_map/reduce_scatter | solution.py:383
  696.9 45.9 %reduce-scatter.23.cloned.1.call-done = f32[3,96,768]{2,1,0:T(8,128)} async-done(((f32[3,768,768]{2,1,0:T(8,128)}), f32[3,96,768]{2,1,0:T(8,128)}) %reduce-scatter.23.cloned.1.call-update) | async-done | bytes 884752 | tf_op jit(solution)/shard_map/reduce_scatter | solution.py:384
  747.2 54.0 %all-reduce.4.cloned.1.call-done = bf16[2,384,768]{1,0,2:T(2,128)(2,1)} async-done(((bf16[2,384,768]{1,0,2:T(2,128)(2,1)}), bf16[2,384,768]{1,0,2:T(2,128)(2,1)}) %all-reduce.4.cloned.1.call-update) | async-done | bytes 1179664
  803.2 29.6 %reduce-scatter.27.cloned.1.call-done = bf16[2,96,768]{2,1,0:T(8,128)(2,1)} async-done(((bf16[2,96,3072]{2,1,0:T(8,128)(2,1)}), bf16[2,96,768]{2,1,0:T(8,128)(2,1)}) %reduce-scatter.27.cloned.1.call-update) | async-done | bytes 294928 | tf_op jit(solution)/shard_map/reduce_scatter | solution.py:398
  832.9 40.1 %reduce-scatter.31.cloned.1.call-done = bf16[576,288]{1,0:T(8,128)(2,1)} async-done(((bf16[2304,288]{1,0:T(8,128)(2,1)}), bf16[576,288]{1,0:T(8,128)(2,1)}) %reduce-scatter.31.cloned.1.call-update) | async-done | bytes 331792
  880.7 28.1 %reduce-scatter.37.cloned.1.call-done = f32[96,5]{1,0:T(8,128)} async-done(((f32[768,5]{1,0:T(8,128)}), f32[96,5]{1,0:T(8,128)}) %reduce-scatter.37.cloned.1.call-update) | async-done | bytes 1936
  909.7 41.5 %reduce-scatter.39.cloned.1.call-done = f32[384,2]{1,0:T(8,128)} async-done(((f32[3072,2]{1,0:T(8,128)}), f32[384,2]{1,0:T(8,128)}) %reduce-scatter.39.cloned.1.call-update) | async-done | bytes 3088
  952.2 35.8 %reduce-scatter.35.cloned.1.call-done = f32[96,16]{1,0:T(8,128)} async-done(((f32[768,16]{1,0:T(8,128)}), f32[96,16]{1,0:T(8,128)}) %reduce-scatter.35.cloned.1.call-update) | async-done | bytes 6160
  988.8 19.5 %all-reduce.1 = (f32[16,96]{1,0:T(8,128)}, f32[5,96]{1,0:T(8,128)}, f32[2,384]{1,0:T(2,128)}) all-reduce(f32[16,96]{1,0:T(8,128)S(1)} %copy.216, f32[5,96]{1,0:T(8,128)S(1)} %copy.218, f32[2,384]{1,0:T(2,128)S(1)} %copy.220), channel_id=1, replica_groups=mesh['rep'=4,'fsdp'=8] {'rep'}, use_global_device_ids=true, to_apply=%region_57.58 | all-reduce | flops 2784 | bytes 22272 | tf_op jit(solution)/shard_map/psum | solution.py:419
  1013.7 23.3 %all_gather.47 = bf16[3,96,768]{1,0,2:T(4,128)(2,1)S(1)} all-gather(bf16[3,96,192]{1,0,2:T(4,128)(2,1)S(1)} %bitcast.368), channel_id=1, replica_groups=mesh['rep'=4,'fsdp'=8] {'rep'}, dimensions={2}, use_global_device_ids=true | all-gather | bytes 552960 | tf_op jit(solution)/shard_map/all_gather | solution.py:409
  1038.3 9.7 all-gather.22.cloned.1.call-done
  1053.1 27.2 %all-gather.20.cloned.1.call-done = bf16[2,96,3072]{2,1,0:T(8,128)(2,1)} async-done(((bf16[2,96,768]{2,1,0:T(8,128)(2,1)}), bf16[2,96,3072]{2,1,0:T(8,128)(2,1)}) %all-gather.20.cloned.1.call-update) | async-done | bytes 1179664 | tf_op jit(solution)/shard_map/all_gather | solution.py:412
  1083.2 48.7 %all-gather.18.cloned.1.call-done = bf16[3,96,2304]{1,0,2:T(4,128)(2,1)} async-done(((bf16[3,96,576]{1,0,2:T(4,128)(2,1)}), bf16[3,96,2304]{1,0,2:T(4,128)(2,1)}) %all-gather.18.cloned.1.call-update) | async-done | bytes 1327120 | tf_op jit(solution)/shard_map/all_gather | solution.py:406
  (580 shorter events, 236.1 us)
Async XLA Ops:
  7.2 69.4 %all-gather.10.cloned.1.call-start = ((), (), s32[]{:S(2)}) async-start(), calls=%async_computation.10 | async-start | bytes 11943936 | tf_op jit(solution)/shard_map/all_gather | solution.py:302
  8.0 104.5 %all-gather.12.cloned.1.call-start = ((), (), s32[]{:S(2)}) async-start(), calls=%async_computation.11 | async-start | bytes 3981312 | tf_op jit(solution)/shard_map/all_gather | solution.py:303
  8.7 164.5 %all-gather.14.cloned.1.call-start = ((), (), s32[]{:S(2)}) async-start(), calls=%async_computation.12 | async-start | bytes 10616832 | tf_op jit(solution)/shard_map/all_gather | solution.py:317
  9.5 224.4 %all-gather.16.cloned.1.call-start = ((), (), s32[]{:S(2)}) async-start(), calls=%async_computation.13 | async-start | bytes 10616832 | tf_op jit(solution)/shard_map/all_gather | solution.py:318
  10.0 393.2 %reduce-scatter.29.cloned.1.call-start = ((), (), s32[]{:S(2)}) async-start(), calls=%async_computation.20 | async-start | bytes 21233664 | tf_op jit(solution)/shard_map/reduce_scatter | solution.py:388
  39.6 205.8 %copy-start.55 = (pred[256,256]{0,1:T(8,128)(4,1)}, pred[256,256]{0,1:T(8,128)(4,1)S(1)}, u32[]{:S(2)}) copy-start(pred[256,256]{0,1:T(8,128)(4,1)S(1)} %broadcast_compare_fusion) | copy-start | bytes 196612
  115.1 131.7 %copy-start.9 = (f32[384,768]{1,0:T(8,128)}, f32[384,768]{1,0:T(8,128)S(1)}, u32[]{:S(2)}) copy-start(f32[384,768]{1,0:T(8,128)S(1)} %multiply_add_fusion) | copy-start | bytes 3538948
  122.2 174.5 %copy-start.133 = (f32[128]{0:T(128)}, f32[128]{0:T(128)S(1)}, u32[]{:S(2)}) copy-start(f32[128]{0:T(128)S(1)} %broadcast_multiply_fusion.15) | copy-start | bytes 1540
  122.5 174.2 %copy-start.136 = (f32[128]{0:T(128)}, f32[128]{0:T(128)S(1)}, u32[]{:S(2)}) copy-start(f32[128]{0:T(128)S(1)} %add_rsqrt_fusion.5) | copy-start | bytes 1540
  277.0 255.9 %reduce-scatter.25.cloned.1.call-start = ((), (), s32[]{:S(2)}) async-start(), calls=%async_computation.17 | async-start | bytes 21233664 | tf_op jit(solution)/shard_map/reduce_scatter | solution.py:387
  313.9 359.8 %reduce-scatter.21.cloned.1.call-start = ((), (), s32[]{:S(2)}) async-start(), calls=%async_computation.14 | async-start | bytes 23887872 | tf_op jit(solution)/shard_map/reduce_scatter | solution.py:383
  391.4 351.4 %reduce-scatter.23.cloned.1.call-start = ((), (), s32[]{:S(2)}) async-start(), calls=%async_computation.16 | async-start | bytes 7962624 | tf_op jit(solution)/shard_map/reduce_scatter | solution.py:384
  398.5 402.7 %all-reduce.4.cloned.1.call-start = ((), (), s32[]{:S(2)}) async-start(), calls=%async_computation.27 | async-start | bytes 2359296
  407.9 424.9 %reduce-scatter.27.cloned.1.call-start = ((), (), s32[]{:S(2)}) async-start(), calls=%async_computation.18 | async-start | bytes 1474560 | tf_op jit(solution)/shard_map/reduce_scatter | solution.py:398
  535.8 337.2 %reduce-scatter.31.cloned.1.call-start = ((), (), s32[]{:S(2)}) async-start(), calls=%async_computation.22 | async-start | bytes 2211840
  684.2 224.7 %reduce-scatter.37.cloned.1.call-start = ((), (), s32[]{:S(2)}) async-start(), calls=%async_computation.25 | async-start | bytes 442368
  693.1 258.1 %reduce-scatter.39.cloned.1.call-start = ((), (), s32[]{:S(2)}) async-start(), calls=%async_computation.26 | async-start | bytes 1769472
  695.4 292.6 %reduce-scatter.35.cloned.1.call-start = ((), (), s32[]{:S(2)}) async-start(), calls=%async_computation.24 | async-start | bytes 442368
  696.8 315.8 %reduce-scatter.33.cloned.1.call-start = ((), (), s32[]{:S(2)}) async-start(), calls=%async_computation.23 | async-start | bytes 737280
  745.8 129.6 %copy-start.87 = (bf16[12,64,128]{2,1,0:T(8,128)(2,1)S(1)}, bf16[12,64,128]{2,1,0:T(8,128)(2,1)}, u32[]{:S(2)}) copy-start(bf16[12,64,128]{2,1,0:T(8,128)(2,1)} %copy-done.86) | copy-start | bytes 589828
  745.8 129.6 %copy-start.89 = (bf16[12,64,128]{2,1,0:T(8,128)(2,1)S(1)}, bf16[12,64,128]{2,1,0:T(8,128)(2,1)}, u32[]{:S(2)}) copy-start(bf16[12,64,128]{2,1,0:T(8,128)(2,1)} %copy-done.88) | copy-start | bytes 589828
  745.9 302.2 %all-gather.22.cloned.1.call-start = ((), (), s32[]{:S(2)}) async-start(), calls=%async_computation.21 | async-start | bytes 1474560 | tf_op jit(solution)/shard_map/all_gather | solution.py:415
  803.1 277.1 %all-gather.20.cloned.1.call-start = ((), (), s32[]{:S(2)}) async-start(), calls=%async_computation.19 | async-start | bytes 1474560 | tf_op jit(solution)/shard_map/all_gather | solution.py:412
  832.8 299.0 %all-gather.18.cloned.1.call-start = ((), (), s32[]{:S(2)}) async-start(), calls=%async_computation.15 | async-start | bytes 2949120 | tf_op jit(solution)/shard_map/all_gather | solution.py:406
  (156 other events, 1465.3 us)
Sparse Core Ops, SparseCore 0:
  9.9 66.6 all-gather.9
  78.5 33.9 all-gather.11
  114.4 58.8 all-gather.13
  175.0 58.8 all-gather.15
  277.1 126.0 reduce-scatter.28
  406.7 126.1 reduce-scatter.24
  536.5 137.1 reduce-scatter.20
  677.2 65.4 reduce-scatter.22
  745.3 55.8 all-reduce.3
  804.0 28.7 reduce-scatter.26
  835.8 37.0 reduce-scatter.30
  875.9 32.9 reduce-scatter.36
  912.7 38.4 reduce-scatter.38
  954.1 33.8 reduce-scatter.34
  990.7 21.9 reduce-scatter.32
  1014.1 33.8 all-gather.21
  1049.4 30.7 all-gather.19
  1082.2 49.5 all-gather.17
where the time goes:
time: 1160 us; the launch traced here: 1140 us
  waiting for transfers between devices  800 us (69%)
  matrix products  105 us (9%)
  local copies, waits for them, and re-layouts  83.7 us (7%)
  blocking collectives  70.2 us (6%)
  other arithmetic  55.4 us (5%)
  between operations  17.6 us (2%)
  starting transfers between devices  13 us (1%)
    unnamed x24, waiting for transfers between devices  207 us
    reduce_scatter x1, waiting for transfers between devices, local(): lax.psum_scatter(inward_grad, 'fsdp', scatter_dimension=1, tiled=True)  138 us
    reduce_scatter x1, waiting for transfers between devices, local(): lax.psum_scatter(expand_grad, 'fsdp', scatter_dimension=1, tiled=True)  125 us
    all_gather x1, waiting for transfers between devices, local(): lax.all_gather(shrink_weight, 'fsdp', axis=1, tiled=True)  52 us
    unnamed x343, local copies, waits for them, and re-layouts  51.2 us
    all_gather x1, waiting for transfers between devices, local(): lax.all_gather(expand_weight, 'fsdp', axis=1, tiled=True)  50.8 us
    all_gather x1, waiting for transfers between devices, local(): lax.all_gather(summed_shares[0].astype(jnp.bfloat16), 'rep', axis=2, tile...  48.7 us
    reduce_scatter x1, waiting for transfers between devices, local(): lax.psum_scatter(outward_grad, 'fsdp', scatter_dimension=1, tiled=True)  45.9 us
  transfers between devices with their start and end apart: 18, of which 18 were waited for; matrix products, arithmetic and copies ran while one was open for 16% of the time, Pallas kernels for 0%

commit v1 on v0

--- a/solution.py
+++ b/solution.py
@@ -1,7 +1,13 @@
+import functools
+
 import jax
 import jax.numpy as jnp
 from jax import lax
+from jax.experimental import pallas as pl
+from jax.experimental.pallas import tpu as pltpu
 from jax.sharding import PartitionSpec as P
+
+MESH = pl.DeviceIdType.MESH
 
 HEADS = 12
 HEAD_DIM = 64
@@ -114,7 +120,7 @@
 def project_back(grad_sum, grad_parts, rows_low, weight):
     width = weight.shape[0]
     grad_mixed = jnp.concatenate(grad_parts, axis=1).astype(jnp.bfloat16)
-    grad_weight = matmul_tn(rows_low, grad_mixed)
+    grad_weight = (rows_low, grad_mixed)
     grad_bias = column_sums(grad_mixed)
     grad_rows = grad_sum + matmul_nt(grad_mixed, weight)
     return (grad_rows, grad_weight, grad_bias[:width], grad_bias[2 * width :])
@@ -123,7 +129,7 @@
 def branch_back(grad_out, context, norm_stats, gain_row, outward_one):
     grad_sum, grad_gain, grad_shift = normalize_back(grad_out, norm_stats, gain_row)
     grad_branch = grad_sum.astype(jnp.bfloat16)
-    grad_outward = matmul_tn(context, grad_branch)
+    grad_outward = (context, grad_branch)
     grad_context = matmul_nt(grad_branch, outward_one).astype(jnp.bfloat16)
     return (grad_sum, grad_context, grad_outward, column_sums(grad_branch), grad_gain, grad_shift)
 
@@ -260,11 +266,11 @@
         grad_out, norm_stats, gain_rows[3 + feed_index]
     )
     grad_branch = grad_sum.astype(jnp.bfloat16)
-    grad_shrink = matmul_tn(hidden, grad_branch)
+    grad_shrink = (hidden, grad_branch)
     grad_hidden = matmul_nt(grad_branch, shrink_all[feed_index])
     unused_value, slope_back = jax.vjp(gelu_exact, before)
     grad_before = slope_back(grad_hidden)[0].astype(jnp.bfloat16)
-    grad_expand = matmul_tn(rows_low, grad_before)
+    grad_expand = (rows_low, grad_before)
     grad_rows = grad_sum + matmul_nt(grad_before, expand_all[feed_index])
     return (
         grad_rows,
@@ -277,7 +283,357 @@
     )
 
 
+UNIT = 96
+WIDE = 768
+SLOTS = 4
+ACC_SLOTS = 6
+LAG_A = 2
+LAG_B = 2
+LAG_Z = 1
+
+
+def grad_kernel(groups, *refs):
+    count = len(groups)
+    lefts = refs[:count]
+    rights = refs[count : 2 * count]
+    small_in = refs[2 * count]
+    out, small_out = refs[2 * count + 1 : 2 * count + 3]
+    (
+        acc,
+        core_out,
+        core_in,
+        half_out,
+        half_in,
+        full_out,
+        full_in,
+        plane,
+        end_out,
+        end_in,
+        mid_out,
+        mid_in,
+        small_in_plane,
+        small_planes,
+        core_send,
+        core_recv,
+        half_send,
+        half_recv,
+        full_send,
+        full_recv,
+        z_send,
+        z_recv,
+        small_send,
+        small_recv,
+        free,
+    ) = refs[2 * count + 3 :]
+    me = lax.axis_index("fsdp")
+    z = lax.axis_index("rep")
+    chip = me // 2
+    lane = me % 2
+    is_end = jnp.logical_or(z == 0, z == 3)
+    is_mid = jnp.logical_or(z == 1, z == 2)
+    xor = lax.bitwise_xor
+    core_peer = {"fsdp": xor(me, 1)}
+    links = ({"fsdp": xor(me, 2)}, {"fsdp": xor(me, 4)})
+    link_chip = (xor(chip, 1), xor(chip, 2))
+    diagonal = xor(chip, 3)
+    pair_peer = {"rep": xor(z, 1)}
+    mid_peer = {"rep": 3 - z}
+    total = sum(group[0] for group in groups)
+
+    barrier = pltpu.get_barrier_semaphore()
+    for offset in range(1, 8):
+        pl.semaphore_signal(barrier, inc=1, device_id={"fsdp": xor(me, offset)}, device_id_type=MESH)
+    for offset in range(1, 4):
+        pl.semaphore_signal(barrier, inc=1, device_id={"rep": (z + offset) % 4}, device_id_type=MESH)
+    pl.semaphore_wait(barrier, 10)
+
+    def remote(src, dst, send_sem, recv_sem, peer):
+        return pltpu.make_async_remote_copy(
+            src_ref=src, dst_ref=dst, send_sem=send_sem, recv_sem=recv_sem, device_id=peer, device_id_type=MESH
+        )
+
+    def small_copy(offset):
+        peer = xor(me, offset)
+        return remote(
+            small_in.at[peer],
+            small_in_plane.at[offset - 1],
+            small_send.at[offset - 1],
+            small_recv.at[offset - 1],
+            {"fsdp": peer},
+        )
+
+    def small_plane_copy(offset):
+        return remote(
+            small_planes.at[z],
+            small_planes.at[z],
+            small_send.at[6 + offset],
+            small_recv.at[6 + offset],
+            {"rep": (z + offset) % 4},
+        )
+
+    for offset in range(1, 8):
+        small_copy(offset).start()
+
+    def core_copy(u):
+        slot = u % SLOTS
+        return remote(core_out.at[slot], core_in.at[slot], core_send.at[slot], core_recv.at[slot], core_peer)
+
+    def half_copy(u, way):
+        slot = u % SLOTS
+        return remote(
+            half_out.at[slot, way], half_in.at[slot, way], half_send.at[slot, way], half_recv.at[slot, way], links[way]
+        )
+
+    def full_copy(u, way):
+        slot = u % SLOTS
+        return remote(
+            full_out.at[slot, way], full_in.at[slot, way], full_send.at[slot, way], full_recv.at[slot, way], links[way]
+        )
+
+    def end_copy(u):
+        slot = u % SLOTS
+        return remote(end_out.at[slot], end_in.at[slot], z_send.at[0, slot], z_recv.at[0, slot], pair_peer)
+
+    def mid_copy(u):
+        slot = u % SLOTS
+        return remote(mid_out.at[slot], mid_in.at[slot], z_send.at[1, slot], z_recv.at[1, slot], mid_peer)
+
+    def back_copy(u):
+        slot = u % SLOTS
+        return remote(out.at[u], out.at[u], z_send.at[2, slot], z_recv.at[2, slot], pair_peer)
+
+    def credit(u, channel, peer):
+        @pl.when(u + SLOTS < total)
+        def _():
+            pl.semaphore_signal(free.at[channel], inc=1, device_id=peer, device_id_type=MESH)
+
+    def spend(u, channel):
+        @pl.when(u >= SLOTS)
+        def _():
+            pl.semaphore_wait(free.at[channel], 1)
+
+    def produce(u):
+        slot = u % SLOTS
+        keep = u % ACC_SLOTS
+        spend(u, 0)
+        first = 0
+        for index, (units, left_step, right_step) in enumerate(groups):
+            start = first
+
+            @pl.when(jnp.logical_and(u >= start, u < start + units))
+            def _(index=index, start=start, left_step=left_step, right_step=right_step):
+                at = u - start
+                left_at = at * left_step
+                column = pl.multiple_of(at * right_step * WIDE, WIDE)
+                right = rights[index][:, pl.ds(column, WIDE)]
+                other = jnp.dot(
+                    lefts[index][left_at * 2 + 1 - lane], right, preferred_element_type=jnp.float32
+                ).astype(jnp.bfloat16)
+                for block in range(4):
+                    core_out[slot, block] = other[block * UNIT : (block + 1) * UNIT]
+                core_copy(u).start()
+                own = jnp.dot(lefts[index][left_at * 2 + lane], right, preferred_element_type=jnp.float32)
+                for block in range(4):
+                    acc[keep, block] = own[block * UNIT : (block + 1) * UNIT]
+
+            first = first + units
+
+    def join_cores(u):
+        slot = u % SLOTS
+        keep = u % ACC_SLOTS
+        core_copy(u).wait()
+        for way in range(2):
+            spend(u, 1 + way)
+        summed = acc[keep, diagonal] + core_in[slot, diagonal].astype(jnp.float32)
+        half_out[slot, 0] = summed[: UNIT // 2].astype(jnp.bfloat16)
+        half_out[slot, 1] = summed[UNIT // 2 :].astype(jnp.bfloat16)
+        for way in range(2):
+            half_copy(u, way).start()
+        for block in (link_chip[0], link_chip[1], chip):
+            acc[keep, block] = acc[keep, block] + core_in[slot, block].astype(jnp.float32)
+        credit(u, 0, core_peer)
+
+    def join_diagonal(u):
+        slot = u % SLOTS
+        keep = u % ACC_SLOTS
+        for way in range(2):
+            half_copy(u, way).wait()
+            spend(u, 3 + way)
+        half = UNIT // 2
+        full_out[slot, 1, :half] = (acc[keep, link_chip[1], :half] + half_in[slot, 0].astype(jnp.float32)).astype(
+            jnp.bfloat16
+        )
+        full_out[slot, 1, half:] = acc[keep, link_chip[1], half:].astype(jnp.bfloat16)
+        full_copy(u, 1).start()
+        full_out[slot, 0, half:] = (acc[keep, link_chip[0], half:] + half_in[slot, 1].astype(jnp.float32)).astype(
+            jnp.bfloat16
+        )
+        full_out[slot, 0, :half] = acc[keep, link_chip[0], :half].astype(jnp.bfloat16)
+        full_copy(u, 0).start()
+        for way in range(2):
+            credit(u, 1 + way, links[way])
+
+    def join_plane(u):
+        slot = u % SLOTS
+        keep = u % ACC_SLOTS
+        for way in range(2):
+            full_copy(u, way).wait()
+        summed = acc[keep, chip] + (full_in[slot, 0].astype(jnp.float32) + full_in[slot, 1].astype(jnp.float32))
+
+        @pl.when(is_end)
+        def _():
+            spend(u, 5)
+            end_out[slot] = summed.astype(jnp.bfloat16)
+            end_copy(u).start()
+
+        @pl.when(is_mid)
+        def _():
+            plane[slot] = summed
+
+        for way in range(2):
+            credit(u, 3 + way, links[way])
+
+    def join_pair(u):
+        slot = u % SLOTS
+
+        @pl.when(is_end)
+        def _():
+            end_copy(u).wait_send()
+
+        @pl.when(is_mid)
+        def _():
+            end_copy(u).wait_recv()
+            spend(u, 6)
+            mid_out[slot] = (plane[slot] + end_in[slot].astype(jnp.float32)).astype(jnp.bfloat16)
+            mid_copy(u).start()
+            credit(u, 5, pair_peer)
+
+    def join_middle(u):
+        slot = u % SLOTS
+
+        @pl.when(is_mid)
+        def _():
+            mid_copy(u).wait()
+            out[u] = (mid_out[slot].astype(jnp.float32) + mid_in[slot].astype(jnp.float32)).astype(jnp.bfloat16)
+            back_copy(u).start()
+            credit(u, 6, mid_peer)
+
+    def finish(u):
+        @pl.when(is_mid)
+        def _():
+            back_copy(u).wait_send()
+
+        @pl.when(is_end)
+        def _():
+            back_copy(u).wait_recv()
+
+    stages = [
+        (0, produce),
+        (1, join_cores),
+        (1 + LAG_A, join_diagonal),
+        (1 + LAG_A + LAG_B, join_plane),
+        (1 + LAG_A + LAG_B + LAG_Z, join_pair),
+        (1 + LAG_A + LAG_B + 2 * LAG_Z, join_middle),
+        (1 + LAG_A + LAG_B + 3 * LAG_Z, finish),
+    ]
+
+    def step(i, carry):
+        for lag, stage in reversed(stages):
+
+            @pl.when(jnp.logical_and(i >= lag, i < total + lag))
+            def _(lag=lag, stage=stage):
+                stage(i - lag)
+
+        @pl.when(i == 2)
+        def _():
+            summed = small_in[me]
+            for offset in range(1, 8):
+                small_copy(offset).wait()
+                summed = summed + small_in_plane[offset - 1]
+            small_planes[z] = summed
+            for offset in range(1, 4):
+                small_plane_copy(offset).start()
+
+        @pl.when(i == 4)
+        def _():
+            for offset in range(1, 4):
+                small_plane_copy(offset).wait_send()
+            for offset in range(1, 4):
+                source = (z + 4 - offset) % 4
+                remote(
+                    small_planes.at[source],
+                    small_planes.at[source],
+                    small_send.at[6 + offset],
+                    small_recv.at[6 + offset],
+                    {"rep": source},
+                ).wait_recv()
+            small_out[...] = small_planes[0] + small_planes[1] + (small_planes[2] + small_planes[3])
+
+        return carry
+
+    lax.fori_loop(0, total + stages[-1][0], step, 0)
+
+
+def sum_grads(groups, lefts, rights, small):
+    total = sum(group[0] for group in groups)
+    block = (UNIT, WIDE)
+    low = jnp.bfloat16
+    dma = pltpu.SemaphoreType.DMA
+    vmem = pl.BlockSpec(memory_space=pltpu.VMEM)
+    return pl.pallas_call(
+        functools.partial(grad_kernel, groups),
+        out_shape=(
+            jax.ShapeDtypeStruct((total,) + block, low),
+            jax.ShapeDtypeStruct(small.shape[1:], jnp.float32),
+        ),
+        in_specs=[vmem] * (2 * len(groups) + 1),
+        out_specs=(vmem, vmem),
+        scratch_shapes=[
+            pltpu.VMEM((ACC_SLOTS, 4) + block, jnp.float32),
+            pltpu.VMEM((SLOTS, 4) + block, low),
+            pltpu.VMEM((SLOTS, 4) + block, low),
+            pltpu.VMEM((SLOTS, 2, UNIT // 2, WIDE), low),
+            pltpu.VMEM((SLOTS, 2, UNIT // 2, WIDE), low),
+            pltpu.VMEM((SLOTS, 2) + block, low),
+            pltpu.VMEM((SLOTS, 2) + block, low),
+            pltpu.VMEM((SLOTS,) + block, jnp.float32),
+            pltpu.VMEM((SLOTS,) + block, low),
+            pltpu.VMEM((SLOTS,) + block, low),
+            pltpu.VMEM((SLOTS,) + block, low),
+            pltpu.VMEM((SLOTS,) + block, low),
+            pltpu.VMEM((7,) + small.shape[1:], jnp.float32),
+            pltpu.VMEM((4,) + small.shape[1:], jnp.float32),
+            dma((SLOTS,)),
+            dma((SLOTS,)),
+            dma((SLOTS, 2)),
+            dma((SLOTS, 2)),
+            dma((SLOTS, 2)),
+            dma((SLOTS, 2)),
+            dma((3, SLOTS)),
+            dma((3, SLOTS)),
+            dma((10,)),
+            dma((10,)),
+            pltpu.SemaphoreType.REGULAR((7,)),
+        ],
+        compiler_params=pltpu.CompilerParams(
+            collective_id=0, has_side_effects=True, vmem_limit_bytes=60 * 2**20
+        ),
+    )(*lefts, *rights, small)
+
+
+def lanes(rows_low):
+    count = rows_low.shape[0]
+    return rows_low.reshape(count, 4, 2, UNIT).transpose(2, 1, 3, 0).reshape(2, 4 * UNIT, count)
+
+
+def hidden_lanes(hidden):
+    count = hidden.shape[0]
+    return hidden.reshape(count, 4, 2, 4, UNIT).transpose(3, 2, 1, 4, 0).reshape(8, 4 * UNIT, count)
+
+
 def local(
+    devices,
+    replicas,
     word_rows,
     region_rows,
     word_segment,
@@ -293,70 +649,52 @@
     region_cotangent,
 ):
     words_count = word_rows.shape[0]
+    width = word_rows.shape[1]
     word_ids = word_segment[0]
     region_ids = region_segment[0]
     cross_mask = word_ids[:, None] == region_ids[None, :]
     word_mask = word_ids[:, None] == word_ids[None, :]
     region_mask = region_ids[:, None] == region_ids[None, :]
-    inward_all, outward_all, bias_all, gain_all = (
+    shard = biases.shape[1]
+    per_shard = hidden_bias.shape[1] // shard
+    small_shard = jnp.concatenate([biases, norm_gain, hidden_bias.reshape(2 * per_shard, shard)], axis=0)
+    small_all = lax.all_gather(small_shard, "fsdp", axis=0)
+    bias_count = biases.shape[0]
+    gain_count = norm_gain.shape[0]
+    row_params = small_all[:, : bias_count + gain_count].transpose(1, 0, 2).reshape(bias_count + gain_count, width)
+    hidden_all = (
+        small_all[:, bias_count + gain_count :]
+        .reshape(devices, 2, per_shard * shard)
+        .transpose(1, 0, 2)
+        .reshape(2, devices * per_shard * shard)
+    )
+    inward_all, outward_all = (
         lax.all_gather(inward, "fsdp", axis=1, tiled=True),
         lax.all_gather(outward, "fsdp", axis=1, tiled=True),
-        lax.all_gather(biases, "fsdp", axis=1, tiled=True),
-        lax.all_gather(norm_gain, "fsdp", axis=1, tiled=True),
     )
     attend_set = (
         inward_all,
         outward_all,
-        bias_all.astype(jnp.float32),
-        gain_all.astype(jnp.float32),
-    )
-    crossed, unused_kept = cross_forward(word_rows, region_rows, attend_set, cross_mask)
+        row_params[:bias_count].astype(jnp.float32),
+        row_params[bias_count:].astype(jnp.float32),
+    )
+    crossed, cross_kept = cross_forward(word_rows, region_rows, attend_set, cross_mask)
     word_one, word_kept = self_forward(crossed[:words_count], attend_set, 1, word_mask)
     region_one, region_kept = self_forward(crossed[words_count:], attend_set, 2, region_mask)
-    expand_all, shrink_all, hidden_all = (
+    expand_all, shrink_all = (
         lax.all_gather(expand_weight, "fsdp", axis=1, tiled=True),
         lax.all_gather(shrink_weight, "fsdp", axis=1, tiled=True),
-        lax.all_gather(hidden_bias, "fsdp", axis=1, tiled=True),
     )
     feed_set = (expand_all, shrink_all, hidden_all)
     word_two, word_feed = feed_forward(word_one, feed_set, 0, attend_set)
     region_two, region_feed = feed_forward(region_one, feed_set, 1, attend_set)
-    expand_again, shrink_again, hidden_again = (
-        lax.all_gather(expand_weight, "fsdp", axis=1, tiled=True),
-        lax.all_gather(shrink_weight, "fsdp", axis=1, tiled=True),
-        lax.all_gather(hidden_bias, "fsdp", axis=1, tiled=True),
-    )
-    feed_later = (expand_again, shrink_again, hidden_again)
-    word_back = feed_backward(
-        word_cotangent.astype(jnp.float32), word_feed, feed_later, 0, attend_set[3]
-    )
-    region_back = feed_backward(
-        region_cotangent.astype(jnp.float32), region_feed, feed_later, 1, attend_set[3]
-    )
-    expand_grad = jnp.stack([word_back[1], region_back[1]])
-    shrink_grad = jnp.stack([word_back[2], region_back[2]])
-    hidden_grad = jnp.stack([word_back[3], region_back[3]])
-    inward_again, outward_again, bias_again, gain_again = (
-        lax.all_gather(inward, "fsdp", axis=1, tiled=True),
-        lax.all_gather(outward, "fsdp", axis=1, tiled=True),
-        lax.all_gather(biases, "fsdp", axis=1, tiled=True),
-        lax.all_gather(norm_gain, "fsdp", axis=1, tiled=True),
-    )
-    attend_later = (
-        inward_again,
-        outward_again,
-        bias_again.astype(jnp.float32),
-        gain_again.astype(jnp.float32),
-    )
-    word_self = self_backward(word_back[0], word_kept, attend_later, 1, word_mask)
-    region_self = self_backward(region_back[0], region_kept, attend_later, 2, region_mask)
-    again_words, again_regions = lax.optimization_barrier((word_rows, region_rows))
-    unused_rows, cross_kept = cross_forward(again_words, again_regions, attend_later, cross_mask)
+    word_back = feed_backward(word_cotangent.astype(jnp.float32), word_feed, feed_set, 0, attend_set[3])
+    region_back = feed_backward(region_cotangent.astype(jnp.float32), region_feed, feed_set, 1, attend_set[3])
+    word_self = self_backward(word_back[0], word_kept, attend_set, 1, word_mask)
+    region_self = self_backward(region_back[0], region_kept, attend_set, 2, region_mask)
     grad_crossed = jnp.concatenate([word_self[0], region_self[0]], axis=0)
-    cross_back = cross_backward(grad_crossed, cross_kept, attend_later, cross_mask, words_count)
-    inward_grad = jnp.stack([cross_back[1], word_self[1], region_self[1]])
-    outward_grad = jnp.stack([cross_back[2], word_self[2], region_self[2]])
-    bias_grad = jnp.stack(
+    cross_back = cross_backward(grad_crossed, cross_kept, attend_set, cross_mask, words_count)
+    row_grads = jnp.stack(
         [
             cross_back[3][0],
             cross_back[3][1],
@@ -374,68 +712,80 @@
             region_back[6],
             word_back[4],
             region_back[4],
+            cross_back[4],
+            word_self[4],
+            region_self[4],
+            word_back[5],
+            region_back[5],
         ]
     )
-    gain_grad = jnp.stack(
-        [cross_back[4], word_self[4], region_self[4], word_back[5], region_back[5]]
-    )
-    inward_part, outward_part, bias_part, gain_part, expand_part, shrink_part, hidden_part = (
-        lax.psum_scatter(inward_grad, "fsdp", scatter_dimension=1, tiled=True),
-        lax.psum_scatter(outward_grad, "fsdp", scatter_dimension=1, tiled=True),
-        lax.psum_scatter(bias_grad, "fsdp", scatter_dimension=1, tiled=True),
-        lax.psum_scatter(gain_grad, "fsdp", scatter_dimension=1, tiled=True),
-        lax.psum_scatter(expand_grad, "fsdp", scatter_dimension=1, tiled=True),
-        lax.psum_scatter(shrink_grad, "fsdp", scatter_dimension=1, tiled=True),
-        lax.psum_scatter(hidden_grad, "fsdp", scatter_dimension=1, tiled=True),
-    )
-    summed_shares = (
-        lax.psum_scatter(
-            inward_part.astype(jnp.bfloat16), "rep", scatter_dimension=2, tiled=True
-        ).astype(jnp.float32),
-        lax.psum_scatter(
-            outward_part.astype(jnp.bfloat16), "rep", scatter_dimension=2, tiled=True
-        ).astype(jnp.float32),
-        lax.psum_scatter(
-            expand_part.astype(jnp.bfloat16), "rep", scatter_dimension=2, tiled=True
-        ).astype(jnp.float32),
-        lax.psum_scatter(
-            shrink_part.astype(jnp.bfloat16), "rep", scatter_dimension=2, tiled=True
-        ).astype(jnp.float32),
-    )
-    matrix_totals = (
-        lax.all_gather(summed_shares[0].astype(jnp.bfloat16), "rep", axis=2, tiled=True).astype(
-            jnp.float32
-        ),
-        lax.all_gather(summed_shares[1].astype(jnp.bfloat16), "rep", axis=2, tiled=True).astype(
-            jnp.float32
-        ),
-        lax.all_gather(summed_shares[2].astype(jnp.bfloat16), "rep", axis=2, tiled=True).astype(
-            jnp.float32
-        ),
-        lax.all_gather(summed_shares[3].astype(jnp.bfloat16), "rep", axis=2, tiled=True).astype(
-            jnp.float32
-        ),
-    )
-    small_totals = lax.psum((bias_part, gain_part, hidden_part), "rep")
+    hidden_grads = jnp.stack([word_back[3], region_back[3]])
+    small_grads = jnp.concatenate(
+        [
+            row_grads.reshape(bias_count + gain_count, devices, shard).transpose(1, 0, 2),
+            hidden_grads.reshape(2, devices, per_shard, shard)
+            .transpose(1, 0, 2, 3)
+            .reshape(devices, 2 * per_shard, shard),
+        ],
+        axis=1,
+    )
+    rows_small = small_grads.shape[1]
+    if devices == 8 and replicas == 4:
+        groups = ((4, 1, 0), (4, 1, 0), (4, 0, 1), (4, 0, 1), (1, 0, 0), (1, 0, 0), (3, 0, 1), (3, 0, 1), (1, 0, 0), (3, 0, 1))
+        pairs = [
+            word_back[2],
+            region_back[2],
+            word_back[1],
+            region_back[1],
+            word_self[2],
+            region_self[2],
+            word_self[1],
+            region_self[1],
+            cross_back[2],
+            cross_back[1],
+        ]
+        lefts = [hidden_lanes(pair[0]) if i < 2 else lanes(pair[0]) for i, pair in enumerate(pairs)]
+        rights = [pair[1] for pair in pairs]
+        padded = jnp.pad(small_grads, ((0, 0), (0, 32 - rows_small), (0, 128 - shard)))
+        units, small_total = sum_grads(groups, lefts, rights, padded)
+        units = units.astype(jnp.float32)
+        small_total = small_total[:rows_small, :shard]
+        shrink_total = units[:8].reshape(2, 4 * UNIT, WIDE)
+        expand_total = units[8:16].reshape(2, 4, UNIT, WIDE).transpose(0, 2, 1, 3).reshape(2, UNIT, 4 * WIDE)
+        outward_total = jnp.stack([units[24], units[16], units[17]])
+        inward_total = (
+            jnp.stack([units[25:28], units[18:21], units[21:24]]).transpose(0, 2, 1, 3).reshape(3, UNIT, 3 * WIDE)
+        )
+    else:
+
+        def reduced(products, axis):
+            mine = lax.psum_scatter(jnp.stack(products), "fsdp", scatter_dimension=axis, tiled=True)
+            return lax.psum(mine.astype(jnp.bfloat16), "rep").astype(jnp.float32)
+
+        shrink_total = reduced([matmul_tn(*word_back[2]), matmul_tn(*region_back[2])], 1)
+        expand_total = reduced([matmul_tn(*word_back[1]), matmul_tn(*region_back[1])], 1)
+        outward_total = reduced([matmul_tn(*cross_back[2]), matmul_tn(*word_self[2]), matmul_tn(*region_self[2])], 1)
+        inward_total = reduced([matmul_tn(*cross_back[1]), matmul_tn(*word_self[1]), matmul_tn(*region_self[1])], 1)
+        small_total = lax.psum(lax.psum_scatter(small_grads, "fsdp", scatter_dimension=0, tiled=False), "rep")
     grad_rows = cross_back[0]
     return (
         word_two.astype(jnp.bfloat16),
         region_two.astype(jnp.bfloat16),
         grad_rows[:words_count],
         grad_rows[words_count:],
-        matrix_totals[0],
-        matrix_totals[1],
-        small_totals[0],
-        small_totals[1],
-        matrix_totals[2],
-        matrix_totals[3],
-        small_totals[2],
+        inward_total,
+        outward_total,
+        small_total[:bias_count],
+        small_total[bias_count : bias_count + gain_count],
+        expand_total,
+        shrink_total,
+        small_total[bias_count + gain_count :].reshape(2, per_shard * shard),
     )
 
 
 def solution(mesh):
     return jax.shard_map(
-        local,
+        functools.partial(local, mesh.shape["fsdp"], mesh.shape["rep"]),
         mesh=mesh,
         in_specs=(
             P(("rep", "fsdp"), None),

time: 1160 us -> 604 us (0.52)
  waiting for transfers between devices: 800 us -> 157 us
  Pallas kernels: 0 us -> 163 us
  blocking collectives: 70.2 us -> 10.7 us
  starting transfers between devices: 13 us -> 0.15 us
    reduce_scatter x5 -> x0, waiting for transfers between devices: 343 us -> none  [the longest x1 138 us: local(): lax.psum_scatter(inward_grad, 'fsdp', scatter_dimension=1, tiled=True)]
    unnamed x24 -> x4, waiting for transfers between devices: 207 us -> 2.58 us
    pallas_call x0 -> x1, Pallas kernels: none -> 163 us  [sum_grads(): pl.pallas_call(functools.partial(grad_kernel, groups), out_shape=(jax.Sha...]
    all_gather x3 -> x0, waiting for transfers between devices: 85.6 us -> none  [the longest x1 48.7 us: local(): lax.all_gather(summed_shares[0].astype(jnp.bfloat16), 'rep', axis=2, tile...]
    unnamed x343 -> x295, local copies, waits for them, and re-layouts: 51.2 us -> 9.24 us
    all_gather x4 -> x1, blocking collectives: 50.7 us -> 10.7 us  [local(): small_all = lax.all_gather(small_shard, 'fsdp', axis=0)]
    another operation x5 -> x2, other arithmetic: 24.8 us -> 1 us  [the longest x1 0.99 us: local(): outward_total = jnp.stack([units[24], units[16], units[17]])]
    psum x1 -> x0, blocking collectives: 19.5 us -> none  [local(): small_totals = lax.psum((bias_part, gain_part, hidden_part), 'rep')]
  transfers between devices with their start and end apart: 18 -> 4, of which waited for: 18 -> 4; matrix products, arithmetic and copies ran while one was open for 16% -> 9% of each run, Pallas kernels for 0% -> 0%
where the time goes in v1:
time: 604 us; the launch traced here: 594 us
  Pallas kernels  163 us (27%)
  waiting for transfers between devices  157 us (26%)
  matrix products  104 us (17%)
  local copies, waits for them, and re-layouts  90.6 us (15%)
  other arithmetic  52.4 us (9%)
  between operations  15.7 us (3%)
  blocking collectives  10.7 us (2%)
    pallas_call x1, Pallas kernels, sum_grads(): pl.pallas_call(functools.partial(grad_kernel, groups), out_shape=(jax.Sha...  163 us
    all_gather x1, waiting for transfers between devices, local(): lax.all_gather(shrink_weight, 'fsdp', axis=1, tiled=True)  49.6 us
    dot_general x10, matrix products, matmul(): return jnp.dot(left_op, right_op, preferred_element_type=jnp.float32)  43.5 us
    all_gather x1, waiting for transfers between devices, local(): lax.all_gather(expand_weight, 'fsdp', axis=1, tiled=True)  41 us
    all_gather x1, waiting for transfers between devices, local(): lax.all_gather(inward, 'fsdp', axis=1, tiled=True)  39.5 us
    dot_general x10, matrix products, matmul_nt(): lax.dot_general(left_op, right_op, (((1,), (1,)), ((), ())), preferred_el...  35.1 us
    all_gather x1, waiting for transfers between devices, local(): lax.all_gather(outward, 'fsdp', axis=1, tiled=True)  24.8 us
    reduce_sum x12, other arithmetic, column_sums(): return jnp.sum(values, axis=0, dtype=jnp.float32)  24 us
  transfers between devices with their start and end apart: 4, of which 4 were waited for; matrix products, arithmetic and copies ran while one was open for 9% of the time, Pallas kernels for 0%

profile of v1, /device:TPU:0, one launch (start us, length us, event | category | flops | bytes accessed | tf_op | source)
XLA Modules:
  0.0 593.9 jit_solution(8581665378241992757)
XLA Ops:
  10.1 10.7 %all-gather.1 = bf16[8,29,96]{2,1,0:T(8,128)(2,1)S(1)} all-gather(bf16[1,29,96]{2,1,0:T(8,128)(2,1)S(1)} %maximum_bitcast_fusion.1), channel_id=2, replica_groups=mesh['rep'=4,'fsdp'=8] {'fsdp'}, dimensions={0}, use_global_device_ids=true | all-gather | bytes 50112 | tf_op jit(solution)/shard_map/all_gather | solution.py:661
  37.0 39.5 %all-gather.7.cloned.1.call-done = bf16[3,768,2304]{2,1,0:T(8,128)(2,1)} async-done(((bf16[3,96,2304]{2,1,0:T(8,128)(2,1)}), bf16[3,768,2304]{2,1,0:T(8,128)(2,1)}) %all-gather.7.cloned.1.call-update) | async-done | bytes 10616848 | tf_op jit(solution)/shard_map/all_gather | solution.py:672
  76.5 3.5 fusion
  87.6 24.8 %all-gather.9.cloned.1.call-done = bf16[3,768,768]{2,1,0:T(8,128)(2,1)} async-done(((bf16[3,96,768]{2,1,0:T(8,128)(2,1)}), bf16[3,768,768]{2,1,0:T(8,128)(2,1)}) %all-gather.9.cloned.1.call-update) | async-done | bytes 3538960 | tf_op jit(solution)/shard_map/all_gather | solution.py:673
  117.2 2.6 fusion.12
  132.2 41.0 %all-gather.11.cloned.1.call-done = bf16[2,768,3072]{2,1,0:T(8,128)(2,1)} async-done(((bf16[2,96,3072]{2,1,0:T(8,128)(2,1)}), bf16[2,768,3072]{2,1,0:T(8,128)(2,1)}) %all-gather.11.cloned.1.call-update) | async-done | bytes 9437200 | tf_op jit(solution)/shard_map/all_gather | solution.py:685
  173.2 8.6 %multiply_convert_fusion.4 = (bf16[128,3072]{1,0:T(8,128)(2,1)}, f32[128,3072]{1,0:T(8,128)}, f32[128,3072]{1,0:T(8,128)}) fusion(f32[3072]{0:T(1024)} %bitcast.367, bf16[128,768]{1,0:T(8,128)(2,1)} %fusion.72, bf16[2,768,3072]{2,1,0:T(8,128)(2,1)} %all-gather.11.cloned.1.call-done), kind=kOutput, calls=%fused_computation.63 | convolution fusion | flops 629932032 | bytes 8859648 | tf_op jit(solution)/shard_map/dot_general | solution.py:21
  184.2 49.6 %all-gather.13.cloned.1.call-done = bf16[2,3072,768]{2,1,0:T(8,128)(2,1)} async-done(((bf16[2,384,768]{2,1,0:T(8,128)(2,1)}), bf16[2,3072,768]{2,1,0:T(8,128)(2,1)}) %all-gather.13.cloned.1.call-update) | async-done | bytes 9437200 | tf_op jit(solution)/shard_map/all_gather | solution.py:686
  233.8 3.6 fusion.108
  239.9 5.7 convert_reduce_fusion.3
  250.3 2.5 convolution_convert_fusion.8
  259.5 3.1 fusion.10
  276.6 12.5 %fusion.60 = bf16[256,768]{1,0:T(8,128)(2,1)} fusion(f32[256,768]{1,0:T(8,128)S(1)} %get-tuple-element.124, f32[768]{0:T(1024)S(1)} %copy-done.97, f32[768]{0:T(1024)S(1)} %copy-done.81, f32[256]{0:T(256)S(1)} %add_rsqrt_fusion.2, f32[256]{0:T(256)S(1)} %broadcast_multiply_fusion.8), kind=kLoop, calls=%fused_computation.173 | loop fusion | flops 983040 | bytes 1187840 | tf_op jit(solution)/shard_map/convert_element_type | solution.py:254
  291.0 11.4 %multiply_convert_fusion.1 = (bf16[256,3072]{1,0:T(8,128)(2,1)}, f32[256,3072]{1,0:T(8,128)}, f32[256,3072]{1,0:T(8,128)}) fusion(f32[3072]{0:T(1024)} %bitcast.366, bf16[256,768]{1,0:T(8,128)(2,1)} %fusion.60, bf16[2,768,3072]{2,1,0:T(8,128)(2,1)} %all-gather.11.cloned.1.call-done), kind=kOutput, calls=%fused_computation.30 | convolution fusion | flops 1259864064 | bytes 12988416 | tf_op jit(solution)/shard_map/dot_general | solution.py:21
  302.4 2.6 copy.194
  305.0 4.7 fusion.110
  312.7 5.3 convert_reduce_fusion.1
  327.4 3.7 convolution_convert_fusion.2
  349.9 4.3 fusion.111
  354.2 4.0 fusion.112
  392.1 8.5 %convert_reduce_fusion = (f32[2304]{0:T(1024)S(1)}, bf16[384,2304]{1,0:T(8,128)(2,1)}) fusion(bf16[256,768]{1,0:T(8,128)(2,1)S(1)} %copy.191, bf16[128,768]{1,0:T(8,128)(2,1)S(1)} %copy.190, bf16[256,768]{1,0:T(8,128)(2,1)S(1)} %copy.188, bf16[128,768]{1,0:T(8,128)(2,1)S(1)} %copy.187, bf16[256,768]{1,0:T(8,128)(2,1)S(1)} %copy.185, ...), kind=kLoop, calls=%fused_computation.24 | loop fusion | flops 12384000 | bytes 3548160 | tf_op jit(solution)/shard_map/reduce_sum | solution.py:37
  401.7 163.4 %shard_map.215 = (bf16[28,96,768]{2,1,0:T(8,128)(2,1)}, f32[32,128]{1,0:T(8,128)}) custom-call(bf16[8,384,128]{2,1,0:T(8,128)(2,1)} %bitcast.302, bf16[8,384,256]{2,1,0:T(8,128)(2,1)} %bitcast.289, bf16[2,384,128]{2,1,0:T(8,128)(2,1)} %bitcast.356, bf16[2,384,256]{2,1,0:T(8,128)(2,1)} %bitcast.330, bf16[2,384,128]{2,1,0:T(8,128)(2,1)} %bitcast.355, ...), custom_call_target="tpu_custom_call" | custom-call | tf_op jit(solution)/shard_map/pallas_call | solution.py:583
  568.4 3.7 fusion.31
  575.8 4.2 convert_element_type.286
  (517 shorter events, 154.6 us)
Async XLA Ops:
  7.2 69.3 %all-gather.7.cloned.1.call-start = ((), (), s32[]{:S(2)}) async-start(), calls=%async_computation | async-start | bytes 11943936 | tf_op jit(solution)/shard_map/all_gather | solution.py:672
  7.9 104.5 %all-gather.9.cloned.1.call-start = ((), (), s32[]{:S(2)}) async-start(), calls=%async_computation.1 | async-start | bytes 3981312 | tf_op jit(solution)/shard_map/all_gather | solution.py:673
  8.7 22.9 %copy-start.73 = (bf16[128,768]{1,0:T(8,128)(2,1)S(1)}, bf16[128,768]{1,0:T(8,128)(2,1)}, u32[]{:S(2)}) copy-start(bf16[128,768]{1,0:T(8,128)(2,1)} %param.13) | copy-start | bytes 589828
  8.7 22.9 %copy-start.66 = (bf16[256,768]{1,0:T(8,128)(2,1)S(1)}, bf16[256,768]{1,0:T(8,128)(2,1)}, u32[]{:S(2)}) copy-start(bf16[256,768]{1,0:T(8,128)(2,1)} %param.14) | copy-start | bytes 1179652
  8.7 164.5 %all-gather.11.cloned.1.call-start = ((), (), s32[]{:S(2)}) async-start(), calls=%async_computation.2 | async-start | bytes 10616832 | tf_op jit(solution)/shard_map/all_gather | solution.py:685
  9.4 224.4 %all-gather.13.cloned.1.call-start = ((), (), s32[]{:S(2)}) async-start(), calls=%async_computation.3 | async-start | bytes 10616832 | tf_op jit(solution)/shard_map/all_gather | solution.py:686
  31.7 44.8 %copy-start.57 = (bf16[384,768]{1,0:T(8,128)(2,1)}, bf16[384,768]{1,0:T(8,128)(2,1)S(1)}, u32[]{:S(2)}) copy-start(bf16[384,768]{1,0:T(8,128)(2,1)S(1)} %constant_dynamic-update-slice_fusion) | copy-start | bytes 1769476
  87.6 27.1 %copy-start.54 = (bf16[12,64,256]{2,1,0:T(8,128)(2,1)}, bf16[12,64,256]{2,1,0:T(8,128)(2,1)S(1)}, u32[]{:S(2)}) copy-start(bf16[12,64,256]{2,1,0:T(8,128)(2,1)S(1)} %convolution_convert_fusion.5) | copy-start | bytes 1179652
  233.8 11.8 %slice-start = ((s8[9437184]{0:T(1024)(128)(4,1)}), s8[4194304]{0:T(1024)(128)(4,1)S(1)}, s32[]{:S(2)}) async-start(s8[9437184]{0:T(1024)(128)(4,1)} %bitcast.371), calls=%async_computation.4 | async-start | bytes 8388608
  233.8 11.8 %slice-start.1 = ((s8[9437184]{0:T(1024)(128)(4,1)}), s8[4194304]{0:T(1024)(128)(4,1)S(1)}, s32[]{:S(2)}) async-start(s8[9437184]{0:T(1024)(128)(4,1)} %bitcast.371), calls=%async_computation.5 | async-start | bytes 8388608
  309.9 8.0 %slice-start.3 = ((s8[9437184]{0:T(1024)(128)(4,1)}), s8[4194304]{0:T(1024)(128)(4,1)S(1)}, s32[]{:S(2)}) async-start(s8[9437184]{0:T(1024)(128)(4,1)} %bitcast.373), calls=%async_computation.7 | async-start | bytes 8388608
  335.7 9.1 %copy-start.50 = (bf16[12,64,256]{2,1,0:T(8,128)(2,1)S(1)}, bf16[12,64,256]{2,1,0:T(8,128)(2,1)}, u32[]{:S(2)}) copy-start(bf16[12,64,256]{2,1,0:T(8,128)(2,1)} %fusion.41) | copy-start | bytes 1179652
  379.5 7.7 %copy-start.88 = (f32[2304]{0:T(1024)S(1)}, f32[2304]{0:T(1024)}, u32[]{:S(2)}) copy-start(f32[2304]{0:T(1024)} %get-tuple-element.67) | copy-start | bytes 27652
  379.5 9.1 %copy-start.10 = (bf16[256,3072]{0,1:T(8,128)(2,1)S(1)}, bf16[256,3072]{0,1:T(8,128)(2,1)}, u32[]{:S(2)}) copy-start(bf16[256,3072]{0,1:T(8,128)(2,1)} %copy.194) | copy-start | bytes 4718596
  392.0 8.8 %copy-start.109 = (f32[1,8,96]{2,0,1:T(1,128)S(1)}, f32[1,8,96]{2,0,1:T(1,128)}, u32[]{:S(2)}) copy-start(f32[1,8,96]{2,0,1:T(1,128)} %stack.107) | copy-start | bytes 9220
  392.0 8.8 %copy-start.110 = (f32[1,8,96]{2,0,1:T(1,128)S(1)}, f32[1,8,96]{2,0,1:T(1,128)}, u32[]{:S(2)}) copy-start(f32[1,8,96]{2,0,1:T(1,128)} %stack.100) | copy-start | bytes 9220
  392.0 8.8 %copy-start.111 = (f32[1,8,96]{2,0,1:T(1,128)S(1)}, f32[1,8,96]{2,0,1:T(1,128)}, u32[]{:S(2)}) copy-start(f32[1,8,96]{2,0,1:T(1,128)} %stack.102) | copy-start | bytes 9220
  392.0 8.8 %copy-start.112 = (f32[1,8,96]{2,0,1:T(1,128)S(1)}, f32[1,8,96]{2,0,1:T(1,128)}, u32[]{:S(2)}) copy-start(f32[1,8,96]{2,0,1:T(1,128)} %stack.105) | copy-start | bytes 9220
  392.0 8.8 %copy-start.113 = (f32[1,8,96]{2,0,1:T(1,128)S(1)}, f32[1,8,96]{2,0,1:T(1,128)}, u32[]{:S(2)}) copy-start(f32[1,8,96]{2,0,1:T(1,128)} %stack.94) | copy-start | bytes 9220
  392.0 8.8 %copy-start.114 = (f32[1,8,96]{2,0,1:T(1,128)S(1)}, f32[1,8,96]{2,0,1:T(1,128)}, u32[]{:S(2)}) copy-start(f32[1,8,96]{2,0,1:T(1,128)} %stack.98) | copy-start | bytes 9220
  392.0 8.8 %copy-start.115 = (f32[1,8,96]{2,0,1:T(1,128)S(1)}, f32[1,8,96]{2,0,1:T(1,128)}, u32[]{:S(2)}) copy-start(f32[1,8,96]{2,0,1:T(1,128)} %stack.93) | copy-start | bytes 9220
  392.0 8.8 %copy-start.116 = (f32[1,8,96]{2,0,1:T(1,128)S(1)}, f32[1,8,96]{2,0,1:T(1,128)}, u32[]{:S(2)}) copy-start(f32[1,8,96]{2,0,1:T(1,128)} %stack.92) | copy-start | bytes 9220
  401.7 166.7 %copy-start.7 = (bf16[384,2304]{1,0:T(8,128)(2,1)S(1)}, bf16[384,2304]{1,0:T(8,128)(2,1)}, u32[]{:S(2)}) copy-start(bf16[384,2304]{1,0:T(8,128)(2,1)} %get-tuple-element.73.refs_19_) | copy-start | bytes 5308420
  401.7 166.7 %copy-start.56 = (f32[384,768]{1,0:T(8,128)S(1)}, f32[384,768]{1,0:T(8,128)}, u32[]{:S(2)}) copy-start(f32[384,768]{1,0:T(8,128)} %get-tuple-element.71) | copy-start | bytes 3538948
  (127 other events, 375.5 us)
Sparse Core Ops, SparseCore 0:
  9.9 66.5 all-gather.6
  78.4 33.9 all-gather.8
  114.3 58.8 all-gather.10
  174.9 58.8 all-gather.12

commit v2 on v1

--- a/solution.py
+++ b/solution.py
@@ -292,12 +292,453 @@
 LAG_Z = 1
 
 
+WORDS = 128
+REGIONS = 256
+ROWS = 384
+HIDDEN = 3072
+PAIRS_OF_HEADS = 6
+PAIR_WIDE = 128
+
+
+def flip(position, bits):
+    return lax.bitwise_xor(position, bits)
+
+
+def dot_nt(left, right):
+    return lax.dot_general(left, right, (((1,), (1,)), ((), ())), preferred_element_type=jnp.float32)
+
+
+def dot_tn(left, right):
+    return lax.dot_general(left, right, (((0,), (0,)), ((), ())), preferred_element_type=jnp.float32)
+
+
+def spread(part):
+    source = lax.broadcasted_iota(jnp.int32, (128, WIDE), 0)
+    target = lax.broadcasted_iota(jnp.int32, (128, WIDE), 1)
+    return jnp.logical_and(source < UNIT, target == source + part * UNIT)
+
+
+def half_lanes():
+    lane = lax.broadcasted_iota(jnp.int32, (1, PAIR_WIDE), 1)
+    return (lane < HEAD_DIM, lane >= HEAD_DIM)
+
+
+def only(values, chosen):
+    return jnp.where(chosen, values, jnp.zeros_like(values))
+
+
+ATTEND_CROSS_WORD = ((0, WORDS), (WORDS, REGIONS))
+ATTEND_CROSS_REGION = ((WORDS, REGIONS), (0, WORDS))
+ATTEND_WORD = ((0, WORDS), (0, WORDS))
+ATTEND_REGION = ((WORDS, REGIONS), (WORDS, REGIONS))
+
+
+def attend_into(rows_of, mixed, allowed, shares, context):
+    (query_at, query_count), (key_at, key_count) = rows_of
+    blocked = jnp.where(allowed, 0.0, masked_score)
+
+    def pair(p, carry):
+        at = pl.multiple_of(p * PAIR_WIDE, PAIR_WIDE)
+        queries = mixed[pl.ds(query_at, query_count), pl.ds(at, PAIR_WIDE)]
+        key_rows = mixed[pl.ds(key_at, key_count), pl.ds(WIDE + at, PAIR_WIDE)]
+        value_rows = mixed[pl.ds(key_at, key_count), pl.ds(2 * WIDE + at, PAIR_WIDE)]
+        total = jnp.zeros((query_count, PAIR_WIDE), jnp.float32)
+        for side, chosen in enumerate(half_lanes()):
+            scores = dot_nt(only(queries, chosen), key_rows) * HEAD_DIM ** (-0.5) + blocked
+            lifted = jnp.exp(scores - jnp.max(scores, axis=-1, keepdims=True))
+            share = (lifted / jnp.sum(lifted, axis=-1, keepdims=True)).astype(jnp.bfloat16)
+            shares[2 * p + side] = share
+            total = total + matmul(share, only(value_rows, chosen))
+        context[pl.ds(query_at, query_count), pl.ds(at, PAIR_WIDE)] = total.astype(jnp.bfloat16)
+        return carry
+
+    lax.fori_loop(0, PAIRS_OF_HEADS, pair, 0)
+
+
+def row_norm(summed):
+    center = summed - jnp.mean(summed, axis=-1, keepdims=True)
+    inverse = lax.rsqrt(jnp.mean(center * center, axis=-1, keepdims=True) + norm_epsilon)
+    return (center * inverse, inverse)
+
+
+def forward_kernel(*refs):
+    (
+        rows_low,
+        word_across,
+        region_across,
+        word_down,
+        region_down,
+        small,
+        inward,
+        outward,
+        expand,
+        shrink,
+        result,
+        params,
+        hidden_rows,
+        mixed_cross,
+        mixed_self,
+        shares_cw,
+        shares_cr,
+        shares_w,
+        shares_r,
+        context_cross_t,
+        context_self_t,
+        rows_zero_t,
+        rows_one_t,
+        rows_two_t,
+        hidden_t,
+        slope,
+        normed,
+        inverse,
+        inward_out,
+        outward_out,
+        expand_out,
+        shrink_out,
+        inward_all,
+        outward_all,
+        expand_all,
+        shrink_all,
+        small_all,
+        stream,
+        stream_low,
+        context,
+        hidden,
+        sends,
+        recvs,
+        small_sends,
+        small_recvs,
+        local_sems,
+    ) = refs
+    me = lax.axis_index("fsdp")
+    peers = {"x": {"fsdp": flip(me, 2)}, "y": {"fsdp": flip(me, 4)}, "core": {"fsdp": flip(me, 1)}}
+
+    barrier = pltpu.get_barrier_semaphore()
+    for offset in range(1, 8):
+        pl.semaphore_signal(barrier, inc=1, device_id={"fsdp": flip(me, offset)}, device_id_type=MESH)
+    pl.semaphore_wait(barrier, 7)
+
+    def remote(src, dst, send_sem, recv_sem, peer):
+        return pltpu.make_async_remote_copy(
+            src_ref=src, dst_ref=dst, send_sem=send_sem, recv_sem=recv_sem, device_id=peer, device_id_type=MESH
+        )
+
+    def small_copy(offset, owner):
+        return remote(
+            small_all.at[owner],
+            small_all.at[owner],
+            small_sends.at[offset - 1],
+            small_recvs.at[offset - 1],
+            {"fsdp": flip(me, offset)},
+        )
+
+    small_all[me] = small[...]
+    for offset in range(1, 8):
+        small_copy(offset, me).start()
+
+    chunks = [
+        (inward, inward_all, 0, 0, UNIT, 0, 3 * WIDE),
+        (outward, outward_all, 0, 0, UNIT, 0, WIDE),
+        (inward, inward_all, 1, 0, UNIT, 0, 3 * WIDE),
+        (inward, inward_all, 2, 0, UNIT, 0, 3 * WIDE),
+        (outward, outward_all, 1, 0, UNIT, 0, WIDE),
+        (outward, outward_all, 2, 0, UNIT, 0, WIDE),
+        (expand, expand_all, 0, 0, UNIT, 0, 2 * WIDE),
+        (expand, expand_all, 0, 0, UNIT, 2 * WIDE, 2 * WIDE),
+        (expand, expand_all, 1, 0, UNIT, 0, 2 * WIDE),
+        (expand, expand_all, 1, 0, UNIT, 2 * WIDE, 2 * WIDE),
+        (shrink, shrink_all, 0, 0, 2 * UNIT, 0, WIDE),
+        (shrink, shrink_all, 0, 2 * UNIT, 2 * UNIT, 0, WIDE),
+        (shrink, shrink_all, 1, 0, 2 * UNIT, 0, WIDE),
+        (shrink, shrink_all, 1, 2 * UNIT, 2 * UNIT, 0, WIDE),
+    ]
+
+    def own_part(k):
+        source, _, matrix, first, count, column, columns = chunks[k]
+        return source.at[matrix, pl.ds(first, count), pl.ds(column, columns)]
+
+    def part(k, owner, half=None):
+        source, gathered, matrix, first, count, column, columns = chunks[k]
+        start = owner * source.shape[1] + first
+        if half is not None:
+            count = count // 2
+            start = start + half * count
+        return gathered.at[matrix, pl.ds(pl.multiple_of(start, 16), count), pl.ds(column, columns)]
+
+    X, Y, DIAG_Y, DIAG_X, CORE_OWN, CORE_X, CORE_Y, CORE_DIAG = range(8)
+
+    def copy(k, kind):
+        owner, half, peer = {
+            X: (me, None, "x"),
+            Y: (me, None, "y"),
+            DIAG_Y: (flip(me, 2), 0, "y"),
+            DIAG_X: (flip(me, 4), 1, "x"),
+            CORE_OWN: (me, None, "core"),
+            CORE_X: (flip(me, 2), None, "core"),
+            CORE_Y: (flip(me, 4), None, "core"),
+            CORE_DIAG: (flip(me, 6), None, "core"),
+        }[kind]
+        source = own_part(k) if kind in (X, Y, CORE_OWN) else part(k, owner, half)
+        return remote(source, part(k, owner, half), sends.at[k, kind], recvs.at[k, kind], peers[peer])
+
+    def arrival(k, kind):
+        owner, half, peer = {
+            X: (flip(me, 2), None, "x"),
+            Y: (flip(me, 4), None, "y"),
+            DIAG_Y: (flip(me, 6), 0, "y"),
+            DIAG_X: (flip(me, 6), 1, "x"),
+            CORE_OWN: (flip(me, 1), None, "core"),
+            CORE_X: (flip(me, 3), None, "core"),
+            CORE_Y: (flip(me, 5), None, "core"),
+            CORE_DIAG: (flip(me, 7), None, "core"),
+        }[kind]
+        here = part(k, owner, half)
+        return remote(here, here, sends.at[k, kind], recvs.at[k, kind], peers[peer])
+
+    def own_local(k):
+        return pltpu.make_async_copy(own_part(k), part(k, me), local_sems.at[k])
+
+    def start_own(k):
+        own_local(k).start()
+        for kind in (X, Y, CORE_OWN):
+            copy(k, kind).start()
+
+    def forward_first(k):
+        arrival(k, X).wait_recv()
+        copy(k, DIAG_Y).start()
+        copy(k, CORE_X).start()
+        arrival(k, Y).wait_recv()
+        copy(k, DIAG_X).start()
+        copy(k, CORE_Y).start()
+
+    def forward_second(k):
+        arrival(k, DIAG_Y).wait_recv()
+        arrival(k, DIAG_X).wait_recv()
+        copy(k, CORE_DIAG).start()
+
+    def complete(k):
+        own_local(k).wait()
+        for kind in (CORE_OWN, CORE_X, CORE_Y, CORE_DIAG):
+            arrival(k, kind).wait_recv()
+
+    keeps = []
+
+    def keep(source, target):
+        saved = pltpu.make_async_copy(source, target, local_sems.at[len(chunks) + len(keeps)])
+        saved.start()
+        keeps.append(saved)
+
+    def read_small():
+        for offset in range(1, 8):
+            small_copy(offset, flip(me, offset)).wait_recv()
+        totals = jnp.zeros((21, WIDE), jnp.float32)
+        hidden_parts = [[jnp.zeros((1, WIDE), jnp.float32) for _ in range(4)] for _ in range(2)]
+        for owner in range(8):
+            own = small_all[owner]
+            totals = totals + matmul(own, spread(owner).astype(jnp.bfloat16))[:21]
+            for q in range(4):
+                placed = matmul(own, spread((owner % 2) * 4 + q).astype(jnp.bfloat16))
+                for f in range(2):
+                    row = 21 + 4 * f + q
+                    hidden_parts[f][owner // 2] = hidden_parts[f][owner // 2] + placed[row : row + 1]
+        params[0:21, :] = totals
+        for f in range(2):
+            for block in range(4):
+                hidden_rows[f : f + 1, block * WIDE : (block + 1) * WIDE] = hidden_parts[f][block]
+
+    def transposed_into(target, values, at, count):
+        target[:, pl.ds(at, count)] = values.T
+
+    def project_into(source, at, count, module, mixed):
+        for third, bias_row in enumerate((3 * module, None, 3 * module + 1)):
+            product = matmul(source[pl.ds(at, count), :], inward_all[module, :, third * WIDE : (third + 1) * WIDE])
+            if bias_row is not None:
+                product = product + params[bias_row : bias_row + 1, :]
+            mixed[pl.ds(at, count), third * WIDE : (third + 1) * WIDE] = product.astype(jnp.bfloat16)
+
+    def join(at, weights, left, residual, bias_row, norm_at, norm_index):
+        rows = pl.ds(at, 128)
+        summed = residual + matmul(left[rows, :], weights) + params[bias_row : bias_row + 1, :]
+        unit, scale = row_norm(summed)
+        normed[norm_at, rows, :] = unit
+        inverse[norm_at, rows, :] = jnp.broadcast_to(scale, (128, 128))
+        return unit * params[16 + norm_index : 17 + norm_index, :] + params[9 + norm_index : 10 + norm_index, :]
+
+    def cross_in():
+        project_into(rows_low, 0, ROWS, 0, mixed_cross)
+        attend_into(ATTEND_CROSS_WORD, mixed_cross, word_down[...] == region_across[...], shares_cw, context)
+        attend_into(ATTEND_CROSS_REGION, mixed_cross, region_down[...] == word_across[...], shares_cr, context)
+        for at in range(0, ROWS, 128):
+            transposed_into(rows_zero_t, rows_low[at : at + 128, :], at, 128)
+            transposed_into(context_cross_t, context[at : at + 128, :], at, 128)
+
+    def cross_out():
+        for at in range(0, ROWS, 128):
+            one = join(at, outward_all[0], context, rows_low[at : at + 128, :].astype(jnp.float32), 2, 0, 0)
+            stream[at : at + 128, :] = one
+            one_low = one.astype(jnp.bfloat16)
+            stream_low[at : at + 128, :] = one_low
+            transposed_into(rows_one_t, one_low, at, 128)
+
+    def word_in():
+        project_into(stream_low, 0, WORDS, 1, mixed_self)
+        attend_into(ATTEND_WORD, mixed_self, word_down[...] == word_across[...], shares_w, context)
+        transposed_into(context_self_t, context[0:WORDS, :], 0, WORDS)
+
+    def region_in():
+        project_into(stream_low, WORDS, REGIONS, 2, mixed_self)
+        attend_into(ATTEND_REGION, mixed_self, region_down[...] == region_across[...], shares_r, context)
+        for at in range(WORDS, ROWS, 128):
+            transposed_into(context_self_t, context[at : at + 128, :], at, 128)
+
+    def self_out(module, first, last):
+        for at in range(first, last, 128):
+            two = join(at, outward_all[module], context, stream[at : at + 128, :], 3 * module + 2, 1, module)
+            stream[at : at + 128, :] = two
+            two_low = two.astype(jnp.bfloat16)
+            stream_low[at : at + 128, :] = two_low
+            transposed_into(rows_two_t, two_low, at, 128)
+
+    def feed_in(f, first, last, column, columns):
+        step = 256
+
+        def tile(t, carry):
+            at = pl.multiple_of(column + t * step, step)
+            for row in range(first, last, 128):
+                before = (
+                    matmul(stream_low[row : row + 128, :], expand_all[f, :, pl.ds(at, step)])
+                    + hidden_rows[f : f + 1, pl.ds(at, step)]
+                )
+                below = 0.5 * (1.0 + lax.erf(before * 0.5**0.5))
+                value = (before * below).astype(jnp.bfloat16)
+                density = jnp.exp(-0.5 * before * before) * 0.3989422804014327
+                hidden[row : row + 128, pl.ds(at, step)] = value
+                hidden_t[pl.ds(at, step), row : row + 128] = value.T
+                slope[row : row + 128, pl.ds(at, step)] = (below + before * density).astype(jnp.bfloat16)
+            return carry
+
+        lax.fori_loop(0, columns // step, tile, 0)
+
+    def feed_out(f, first, last):
+        for at in range(first, last, 128):
+            last_rows = join(at, shrink_all[f], hidden, stream[at : at + 128, :], 14 + f, 2, 3 + f)
+            result[at : at + 128, :] = last_rows.astype(jnp.bfloat16)
+
+    def nothing():
+        pass
+
+    pieces = [
+        lambda: (cross_in(), keep(inward_all.at[0], inward_out.at[0])),
+        lambda: (cross_out(), keep(outward_all.at[0], outward_out.at[0])),
+        lambda: (word_in(), keep(inward_all.at[1], inward_out.at[1])),
+        lambda: (region_in(), keep(inward_all.at[2], inward_out.at[2])),
+        lambda: (self_out(1, 0, WORDS), keep(outward_all.at[1], outward_out.at[1])),
+        lambda: (self_out(2, WORDS, ROWS), keep(outward_all.at[2], outward_out.at[2])),
+        lambda: feed_in(0, 0, WORDS, 0, 2 * WIDE),
+        lambda: (feed_in(0, 0, WORDS, 2 * WIDE, 2 * WIDE), keep(expand_all.at[0], expand_out.at[0])),
+        lambda: feed_in(1, WORDS, ROWS, 0, 2 * WIDE),
+        lambda: (feed_in(1, WORDS, ROWS, 2 * WIDE, 2 * WIDE), keep(expand_all.at[1], expand_out.at[1])),
+        nothing,
+        lambda: (keep(shrink_all.at[0], shrink_out.at[0]), feed_out(0, 0, WORDS)),
+        nothing,
+        lambda: (keep(shrink_all.at[1], shrink_out.at[1]), feed_out(1, WORDS, ROWS)),
+    ]
+    count = len(chunks)
+    start_own(0)
+    start_own(1)
+    read_small()
+    for k in range(count + 2):
+        if k + 2 < count:
+            start_own(k + 2)
+        if k < count:
+            forward_first(k)
+        if 0 <= k - 1 < count:
+            forward_second(k - 1)
+        if 0 <= k - 2 < count:
+            complete(k - 2)
+            pieces[k - 2]()
+    for saved in keeps:
+        saved.wait()
+    for offset in range(1, 8):
+        small_copy(offset, me).wait_send()
+    for k in range(count):
+        for kind in range(8):
+            copy(k, kind).wait_send()
+
+
+def forward(rows_low, word_ids, region_ids, small, inward, outward, expand, shrink):
+    low = jnp.bfloat16
+    dma = pltpu.SemaphoreType.DMA
+    vmem = pl.BlockSpec(memory_space=pltpu.VMEM)
+    hbm = pl.BlockSpec(memory_space=pl.ANY)
+    shape = jax.ShapeDtypeStruct
+    weights = [
+        shape((3, WIDE, 3 * WIDE), low),
+        shape((3, WIDE, WIDE), low),
+        shape((2, WIDE, HIDDEN), low),
+        shape((2, HIDDEN, WIDE), low),
+    ]
+    residuals = [
+        shape((24, WIDE), jnp.float32),
+        shape((2, HIDDEN), jnp.float32),
+        shape((ROWS, 3 * WIDE), low),
+        shape((ROWS, 3 * WIDE), low),
+        shape((HEADS, WORDS, REGIONS), low),
+        shape((HEADS, REGIONS, WORDS), low),
+        shape((HEADS, WORDS, WORDS), low),
+        shape((HEADS, REGIONS, REGIONS), low),
+        shape((WIDE, ROWS), low),
+        shape((WIDE, ROWS), low),
+        shape((WIDE, ROWS), low),
+        shape((WIDE, ROWS), low),
+        shape((WIDE, ROWS), low),
+        shape((HIDDEN, ROWS), low),
+        shape((ROWS, HIDDEN), low),
+        shape((3, ROWS, WIDE), jnp.float32),
+        shape((3, ROWS, 128), jnp.float32),
+    ]
+    out_shape = [shape((ROWS, WIDE), low)] + residuals + weights
+    outs = pl.pallas_call(
+        forward_kernel,
+        out_shape=out_shape,
+        in_specs=[vmem] * 6 + [hbm] * 4,
+        out_specs=[vmem] * (1 + len(residuals)) + [hbm] * 4,
+        scratch_shapes=[pltpu.VMEM(w.shape, w.dtype) for w in weights]
+        + [
+            pltpu.VMEM((8, 32, 128), low),
+            pltpu.VMEM((ROWS, WIDE), jnp.float32),
+            pltpu.VMEM((ROWS, WIDE), low),
+            pltpu.VMEM((ROWS, WIDE), low),
+            pltpu.VMEM((ROWS, HIDDEN), low),
+            dma((14, 8)),
+            dma((14, 8)),
+            dma((7,)),
+            dma((7,)),
+            dma((24,)),
+        ],
+        compiler_params=pltpu.CompilerParams(
+            collective_id=1, has_side_effects=True, vmem_limit_bytes=64 * 2**20 - 2**16
+        ),
+    )(
+        rows_low,
+        word_ids,
+        region_ids,
+        word_ids.reshape(WORDS, 1),
+        region_ids.reshape(REGIONS, 1),
+        small,
+        inward,
+        outward,
+        expand,
+        shrink,
+    )
+    return outs[0], outs[1 : 1 + len(residuals)], outs[1 + len(residuals) :]
+
+
 def grad_kernel(groups, *refs):
-    count = len(groups)
-    lefts = refs[:count]
-    rights = refs[count : 2 * count]
-    small_in = refs[2 * count]
-    out, small_out = refs[2 * count + 1 : 2 * count + 3]
+    lefts = refs[:6]
+    rights = refs[6:12]
+    small_in = refs[12]
+    out, small_out = refs[13:15]
     (
         acc,
         core_out,
@@ -324,7 +765,7 @@
         small_send,
         small_recv,
         free,
-    ) = refs[2 * count + 3 :]
+    ) = refs[15:]
     me = lax.axis_index("fsdp")
     z = lax.axis_index("rep")
     chip = me // 2
@@ -417,22 +858,28 @@
         keep = u % ACC_SLOTS
         spend(u, 0)
         first = 0
-        for index, (units, left_step, right_step) in enumerate(groups):
+        for units, side, first_row, rows, by_row in groups:
             start = first
 
             @pl.when(jnp.logical_and(u >= start, u < start + units))
-            def _(index=index, start=start, left_step=left_step, right_step=right_step):
+            def _(start=start, side=side, rows=pl.ds(first_row, rows), by_row=by_row):
                 at = u - start
-                left_at = at * left_step
-                column = pl.multiple_of(at * right_step * WIDE, WIDE)
-                right = rights[index][:, pl.ds(column, WIDE)]
-                other = jnp.dot(
-                    lefts[index][left_at * 2 + 1 - lane], right, preferred_element_type=jnp.float32
-                ).astype(jnp.bfloat16)
+                column = 0 if by_row else pl.multiple_of(at * WIDE, WIDE)
+                right = rights[side][rows, pl.ds(column, WIDE)]
+
+                def product(core):
+                    blocks = []
+                    for block in range(4):
+                        owner = 2 * block + core
+                        row = owner * (4 * UNIT) + at * UNIT if by_row else owner * UNIT
+                        blocks.append(lefts[side][pl.ds(pl.multiple_of(row, 16), UNIT), rows])
+                    return matmul(jnp.concatenate(blocks, axis=0), right)
+
+                other = product(1 - lane).astype(jnp.bfloat16)
                 for block in range(4):
                     core_out[slot, block] = other[block * UNIT : (block + 1) * UNIT]
                 core_copy(u).start()
-                own = jnp.dot(lefts[index][left_at * 2 + lane], right, preferred_element_type=jnp.float32)
+                own = product(lane)
                 for block in range(4):
                     acc[keep, block] = own[block * UNIT : (block + 1) * UNIT]
 
@@ -586,7 +1033,7 @@
             jax.ShapeDtypeStruct((total,) + block, low),
             jax.ShapeDtypeStruct(small.shape[1:], jnp.float32),
         ),
-        in_specs=[vmem] * (2 * len(groups) + 1),
+        in_specs=[vmem] * (len(lefts) + len(rights) + 1),
         out_specs=(vmem, vmem),
         scratch_shapes=[
             pltpu.VMEM((ACC_SLOTS, 4) + block, jnp.float32),
@@ -621,19 +1068,201 @@
     )(*lefts, *rights, small)
 
 
-def lanes(rows_low):
-    count = rows_low.shape[0]
-    return rows_low.reshape(count, 4, 2, UNIT).transpose(2, 1, 3, 0).reshape(2, 4 * UNIT, count)
-
-
-def hidden_lanes(hidden):
-    count = hidden.shape[0]
-    return hidden.reshape(count, 4, 2, 4, UNIT).transpose(3, 2, 1, 4, 0).reshape(8, 4 * UNIT, count)
-
-
-def local(
+GROUPS = (
+    (4, 0, 0, WORDS, True),
+    (4, 0, WORDS, REGIONS, True),
+    (4, 1, 0, WORDS, False),
+    (4, 1, WORDS, REGIONS, False),
+    (1, 2, 0, WORDS, False),
+    (1, 2, WORDS, REGIONS, False),
+    (3, 3, 0, WORDS, False),
+    (3, 3, WORDS, REGIONS, False),
+    (1, 4, 0, ROWS, False),
+    (3, 5, 0, ROWS, False),
+)
+
+
+def shares_back(shares, queries, key_rows, value_rows, grad_context):
+    grad_heads = heads_of(grad_context)
+    grad_shares = jnp.einsum(
+        "qhd,khd->hqk", grad_heads, heads_of(value_rows), preferred_element_type=jnp.float32
+    )
+    grad_values = jnp.einsum("hqk,qhd->khd", shares, grad_heads, preferred_element_type=jnp.float32)
+    wide = shares.astype(jnp.float32)
+    grad_scores = (wide * (grad_shares - jnp.sum(wide * grad_shares, axis=-1, keepdims=True))).astype(jnp.bfloat16)
+    score_scale = HEAD_DIM ** (-0.5)
+    grad_queries = score_scale * jnp.einsum(
+        "hqk,khd->qhd", grad_scores, heads_of(key_rows), preferred_element_type=jnp.float32
+    )
+    grad_keys = score_scale * jnp.einsum(
+        "hqk,qhd->khd", grad_scores, heads_of(queries), preferred_element_type=jnp.float32
+    )
+    return (merge_heads(grad_queries), merge_heads(grad_keys), merge_heads(grad_values))
+
+
+def thirds(mixed):
+    return (mixed[:, :WIDE], mixed[:, WIDE : 2 * WIDE], mixed[:, 2 * WIDE :])
+
+
+def paired(
+    word_rows,
+    region_rows,
+    word_segment,
+    region_segment,
+    inward,
+    outward,
+    biases,
+    norm_gain,
+    expand_weight,
+    shrink_weight,
+    hidden_bias,
+    word_cotangent,
+    region_cotangent,
+):
+    small = jnp.concatenate([biases, norm_gain, hidden_bias.reshape(8, UNIT)], axis=0)
+    small = jnp.pad(small, ((0, 3), (0, 128 - UNIT)))
+    rows_low = jnp.concatenate([word_rows, region_rows], axis=0)
+    result, residuals, weights = forward(
+        rows_low, word_segment, region_segment, small, inward, outward, expand_weight, shrink_weight
+    )
+    (
+        params,
+        hidden_rows,
+        mixed_cross,
+        mixed_self,
+        shares_cw,
+        shares_cr,
+        shares_w,
+        shares_r,
+        context_cross_t,
+        context_self_t,
+        rows_zero_t,
+        rows_one_t,
+        rows_two_t,
+        hidden_t,
+        slope,
+        normed,
+        inverse,
+    ) = residuals
+    inward_all, outward_all, expand_all, shrink_all = weights
+    gains = params[16:21]
+    cut = WORDS
+    low = jnp.bfloat16
+    f32 = jnp.float32
+
+    def norm_back(grad_out, kind, index, first, last):
+        return normalize_back(
+            grad_out[first:last], (normed[kind, first:last], inverse[kind, first:last, :1]), gains[index]
+        )
+
+    def two(function):
+        return (function(0, 0, cut), function(1, cut, ROWS))
+
+    cotangent = jnp.concatenate([word_cotangent, region_cotangent], axis=0).astype(f32)
+    feed = two(lambda f, first, last: norm_back(cotangent, 2, 3 + f, first, last))
+    grad_sum = jnp.concatenate([feed[0][0], feed[1][0]], axis=0)
+    grad_end = grad_sum.astype(low)
+    grad_before = jnp.concatenate(
+        two(
+            lambda f, first, last: (
+                matmul_nt(grad_end[first:last], shrink_all[f]) * slope[first:last].astype(f32)
+            ).astype(low)
+        ),
+        axis=0,
+    )
+    grad_two = grad_sum + jnp.concatenate(
+        two(lambda f, first, last: matmul_nt(grad_before[first:last], expand_all[f])), axis=0
+    )
+    own = two(lambda f, first, last: norm_back(grad_two, 1, 1 + f, first, last))
+    grad_sum_one = jnp.concatenate([own[0][0], own[1][0]], axis=0)
+    grad_self = grad_sum_one.astype(low)
+    grad_context = jnp.concatenate(
+        two(lambda f, first, last: matmul_nt(grad_self[first:last], outward_all[1 + f])), axis=0
+    ).astype(low)
+    self_parts = two(
+        lambda f, first, last: jnp.concatenate(
+            shares_back((shares_w, shares_r)[f], *thirds(mixed_self[first:last]), grad_context[first:last]), axis=1
+        ).astype(low)
+    )
+    grad_mixed_self = jnp.concatenate(self_parts, axis=0)
+    grad_one = grad_sum_one + jnp.concatenate(
+        two(lambda f, first, last: matmul_nt(grad_mixed_self[first:last], inward_all[1 + f])), axis=0
+    )
+    crossed = norm_back(grad_one, 0, 0, 0, ROWS)
+    grad_cross = crossed[0].astype(low)
+    grad_context_cross = matmul_nt(grad_cross, outward_all[0]).astype(low)
+    word_mix, region_mix = thirds(mixed_cross[:cut]), thirds(mixed_cross[cut:])
+    from_words = shares_back(shares_cw, word_mix[0], region_mix[1], region_mix[2], grad_context_cross[:cut])
+    from_regions = shares_back(shares_cr, region_mix[0], word_mix[1], word_mix[2], grad_context_cross[cut:])
+    grad_mixed_cross = jnp.concatenate(
+        [
+            jnp.concatenate([from_words[0], from_regions[1], from_regions[2]], axis=1),
+            jnp.concatenate([from_regions[0], from_words[1], from_words[2]], axis=1),
+        ],
+        axis=0,
+    ).astype(low)
+    grad_rows = crossed[0] + matmul_nt(grad_mixed_cross, inward_all[0])
+
+    ends = two(lambda f, first, last: column_sums(grad_end[first:last]))
+    hidden_grads = two(lambda f, first, last: column_sums(grad_before[first:last]))
+    self_bias = two(lambda f, first, last: column_sums(grad_mixed_self[first:last]))
+    self_ends = two(lambda f, first, last: column_sums(grad_self[first:last]))
+    cross_bias = column_sums(grad_mixed_cross)
+    row_grads = jnp.stack(
+        [
+            cross_bias[:WIDE],
+            cross_bias[2 * WIDE :],
+            column_sums(grad_cross),
+            self_bias[0][:WIDE],
+            self_bias[0][2 * WIDE :],
+            self_ends[0],
+            self_bias[1][:WIDE],
+            self_bias[1][2 * WIDE :],
+            self_ends[1],
+            crossed[2],
+            own[0][2],
+            own[1][2],
+            feed[0][2],
+            feed[1][2],
+            ends[0],
+            ends[1],
+            crossed[1],
+            own[0][1],
+            own[1][1],
+            feed[0][1],
+            feed[1][1],
+        ]
+    )
+    small_grads = jnp.concatenate(
+        [
+            row_grads.reshape(21, 8, UNIT).transpose(1, 0, 2),
+            jnp.stack(hidden_grads).reshape(2, 8, 4, UNIT).transpose(1, 0, 2, 3).reshape(8, 8, UNIT),
+        ],
+        axis=1,
+    )
+    padded = jnp.pad(small_grads, ((0, 0), (0, 3), (0, 128 - UNIT)))
+    lefts = [hidden_t, rows_two_t, context_self_t, rows_one_t, context_cross_t, rows_zero_t]
+    rights = [grad_end, grad_before, grad_self, grad_mixed_self, grad_cross, grad_mixed_cross]
+    units, small_total = sum_grads(GROUPS, lefts, rights, padded)
+    units = units.astype(f32)
+    small_total = small_total[:, :UNIT]
+    return (
+        result[:cut],
+        result[cut:],
+        grad_rows[:cut],
+        grad_rows[cut:],
+        jnp.stack([units[25:28], units[18:21], units[21:24]]).transpose(0, 2, 1, 3).reshape(3, UNIT, 3 * WIDE),
+        jnp.stack([units[24], units[16], units[17]]),
+        small_total[:16],
+        small_total[16:21],
+        units[8:16].reshape(2, 4, UNIT, WIDE).transpose(0, 2, 1, 3).reshape(2, UNIT, 4 * WIDE),
+        units[:8].reshape(2, 4 * UNIT, WIDE),
+        small_total[21:29].reshape(2, 4 * UNIT),
+    )
+
+
+def general(
     devices,
-    replicas,
     word_rows,
     region_rows,
     word_segment,
@@ -729,44 +1358,16 @@
         ],
         axis=1,
     )
-    rows_small = small_grads.shape[1]
-    if devices == 8 and replicas == 4:
-        groups = ((4, 1, 0), (4, 1, 0), (4, 0, 1), (4, 0, 1), (1, 0, 0), (1, 0, 0), (3, 0, 1), (3, 0, 1), (1, 0, 0), (3, 0, 1))
-        pairs = [
-            word_back[2],
-            region_back[2],
-            word_back[1],
-            region_back[1],
-            word_self[2],
-            region_self[2],
-            word_self[1],
-            region_self[1],
-            cross_back[2],
-            cross_back[1],
-        ]
-        lefts = [hidden_lanes(pair[0]) if i < 2 else lanes(pair[0]) for i, pair in enumerate(pairs)]
-        rights = [pair[1] for pair in pairs]
-        padded = jnp.pad(small_grads, ((0, 0), (0, 32 - rows_small), (0, 128 - shard)))
-        units, small_total = sum_grads(groups, lefts, rights, padded)
-        units = units.astype(jnp.float32)
-        small_total = small_total[:rows_small, :shard]
-        shrink_total = units[:8].reshape(2, 4 * UNIT, WIDE)
-        expand_total = units[8:16].reshape(2, 4, UNIT, WIDE).transpose(0, 2, 1, 3).reshape(2, UNIT, 4 * WIDE)
-        outward_total = jnp.stack([units[24], units[16], units[17]])
-        inward_total = (
-            jnp.stack([units[25:28], units[18:21], units[21:24]]).transpose(0, 2, 1, 3).reshape(3, UNIT, 3 * WIDE)
-        )
-    else:
-
-        def reduced(products, axis):
-            mine = lax.psum_scatter(jnp.stack(products), "fsdp", scatter_dimension=axis, tiled=True)
-            return lax.psum(mine.astype(jnp.bfloat16), "rep").astype(jnp.float32)
-
-        shrink_total = reduced([matmul_tn(*word_back[2]), matmul_tn(*region_back[2])], 1)
-        expand_total = reduced([matmul_tn(*word_back[1]), matmul_tn(*region_back[1])], 1)
-        outward_total = reduced([matmul_tn(*cross_back[2]), matmul_tn(*word_self[2]), matmul_tn(*region_self[2])], 1)
-        inward_total = reduced([matmul_tn(*cross_back[1]), matmul_tn(*word_self[1]), matmul_tn(*region_self[1])], 1)
-        small_total = lax.psum(lax.psum_scatter(small_grads, "fsdp", scatter_dimension=0, tiled=False), "rep")
+
+    def reduced(products, axis):
+        mine = lax.psum_scatter(jnp.stack(products), "fsdp", scatter_dimension=axis, tiled=True)
+        return lax.psum(mine.astype(jnp.bfloat16), "rep").astype(jnp.float32)
+
+    shrink_total = reduced([matmul_tn(*word_back[2]), matmul_tn(*region_back[2])], 1)
+    expand_total = reduced([matmul_tn(*word_back[1]), matmul_tn(*region_back[1])], 1)
+    outward_total = reduced([matmul_tn(*cross_back[2]), matmul_tn(*word_self[2]), matmul_tn(*region_self[2])], 1)
+    inward_total = reduced([matmul_tn(*cross_back[1]), matmul_tn(*word_self[1]), matmul_tn(*region_self[1])], 1)
+    small_total = lax.psum(lax.psum_scatter(small_grads, "fsdp", scatter_dimension=0, tiled=False), "rep")
     grad_rows = cross_back[0]
     return (
         word_two.astype(jnp.bfloat16),
@@ -784,8 +1385,9 @@
 
 
 def solution(mesh):
+    sizes = (mesh.shape["rep"], mesh.shape["fsdp"])
     return jax.shard_map(
-        functools.partial(local, mesh.shape["fsdp"], mesh.shape["rep"]),
+        paired if sizes == (4, 8) else functools.partial(general, mesh.shape["fsdp"]),
         mesh=mesh,
         in_specs=(
             P(("rep", "fsdp"), None),

time: 604 us -> 553 us (0.916)
  waiting for transfers between devices: 157 us -> 0 us
  Pallas kernels: 163 us -> 319 us
  matrix products: 104 us -> 66.3 us
  local copies, waits for them, and re-layouts: 90.6 us -> 112 us
  between operations: 15.7 us -> 1.73 us
  blocking collectives: 10.7 us -> 0 us
  other arithmetic: 52.4 us -> 44.5 us
    all_gather x4 -> x0, waiting for transfers between devices: 155 us -> none  [the longest x1 49.6 us: local(): lax.all_gather(shrink_weight, 'fsdp', axis=1, tiled=True)]
    pallas_call x0 -> x1, Pallas kernels: none -> 154 us  [forward(): pl.pallas_call(forward_kernel, out_shape=out_shape, in_specs=[vmem] * 6 +...]
    dot_general x34 -> x16, matrix products: 68.4 us -> 24.7 us  [the longest x4 9.3 us: shares_back(): jnp.einsum('hqk,qhd->khd', shares, grad_heads, preferred_element_type=jnp...]
    slice x36 -> x37, local copies, waits for them, and re-layouts: 25.3 us -> 56.9 us  [the longest x14 27.1 us: thirds(): return (mixed[:, :WIDE], mixed[:, WIDE:2 * WIDE], mixed[:, 2 * WIDE:])]
    convert_element_type x10 -> x7, other arithmetic: 20.1 us -> 2.59 us  [the longest x4 1.48 us: shares_back(): (wide * (grad_shares - jnp.sum(wide * grad_shares, axis=-1, keepdims=True...]
    convert_element_type x10 -> x0, local copies, waits for them, and re-layouts: 14.6 us -> none  [the longest x2 4.99 us: feed_forward(): hidden = gelu_exact(before).astype(jnp.bfloat16)]
    reshape x12, local copies, waits for them, and re-layouts: 11 us -> 21.9 us  [merge_heads(): return head_rows.reshape(head_rows.shape[0], -1)]
    all_gather x1 -> x0, blocking collectives: 10.7 us -> none  [local(): small_all = lax.all_gather(small_shard, 'fsdp', axis=0)]
  transfers between devices with their start and end apart: 4 -> 0, of which waited for: 4 -> 0; matrix products, arithmetic and copies ran while one was open for 9% -> 0% of each run, Pallas kernels for 0% -> 0%
where the time goes in v2:
time: 553 us; the launch traced here: 544 us
  Pallas kernels  319 us (58%)
  local copies, waits for them, and re-layouts  112 us (20%)
  matrix products  66.3 us (12%)
  other arithmetic  44.5 us (8%)
    pallas_call x1, Pallas kernels, sum_grads(): pl.pallas_call(functools.partial(grad_kernel, groups), out_shape=(jax.Sha...  165 us
    pallas_call x1, Pallas kernels, forward(): pl.pallas_call(forward_kernel, out_shape=out_shape, in_specs=[vmem] * 6 +...  154 us
    dot_general x10, matrix products, matmul_nt(): lax.dot_general(left_op, right_op, (((1,), (1,)), ((), ())), preferred_el...  41.6 us
    slice x14, local copies, waits for them, and re-layouts, thirds(): return (mixed[:, :WIDE], mixed[:, WIDE:2 * WIDE], mixed[:, 2 * WIDE:])  27.1 us
    reshape x12, local copies, waits for them, and re-layouts, merge_heads(): return head_rows.reshape(head_rows.shape[0], -1)  21.9 us
    reduce_sum x13, other arithmetic, column_sums(): return jnp.sum(values, axis=0, dtype=jnp.float32)  18.4 us
    another operation x22, local copies, waits for them, and re-layouts, paired(): jnp.stack([cross_bias[:WIDE], cross_bias[2 * WIDE:], column_sums(grad_cro...  15.2 us

profile of v2, /device:TPU:0, one launch (start us, length us, event | category | flops | bytes accessed | tf_op | source)
XLA Modules:
  0.0 543.6 jit_solution(10906461635139815669)
XLA Ops:
  7.5 154.3 %shard_map.212 = (bf16[384,768]{1,0:T(8,128)(2,1)}, f32[24,768]{1,0:T(8,128)}, f32[2,3072]{1,0:T(2,128)}, bf16[384,2304]{1,0:T(8,128)(2,1)}, bf16[384,2304]{1,0:...) custom-call(bf16[384,768]{1,0:T(8,128)(2,1)} %pad_maximum_fusion.5.r, ...), custom_call_target="tpu_custom_call" | custom-call | tf_op jit(solution)/shard_map/pallas_call | solution.py:701
  168.4 2.3 fusion.79
  176.6 2.3 fusion.93
  188.3 5.9 %convert_reduce_fusion.3 = (f32[3072]{0:T(1024)}, bf16[128,3072]{1,0:T(8,128)(2,1)}) fusion(bf16[384,3072]{1,0:T(8,128)(2,1)} %get-tuple-element.39, bf16[2,3072,768]{2,1,0:T(8,128)(2,1)} %get-tuple-element.38, bf16[384,768]{1,0:T(8,128)(2,1)} %copy-done.11), kind=kOutput, calls=%fused_computation.44 | convolution fusion | flops 605942784 | bytes 6500352 | tf_op jit(solution)/shard_map/dot_general | solution.py:31
  194.1 5.5 %convert_reduce_fusion.1 = (f32[3072]{0:T(1024)}, bf16[256,3072]{1,0:T(8,128)(2,1)}) fusion(bf16[384,3072]{1,0:T(8,128)(2,1)S(1)} %copy-done.54, bf16[2,3072,768]{2,1,0:T(8,128)(2,1)} %get-tuple-element.38, bf16[384,768]{1,0:T(8,128)(2,1)S(1)} %copy-done.12), kind=kOutput, calls=%fused_computation.30 | convolution fusion | flops 1211888640 | bytes 8269824 | tf_op jit(solution)/shard_map/dot_general | solution.py:31
  203.2 4.4 fusion.4
  207.6 3.8 fusion
  230.9 2.6 fusion.62
  235.2 2.0 convolution_convert_fusion.5
  239.0 2.6 convolution_convert_fusion.3
  243.6 2.8 convolution_convert_fusion.2
  248.3 2.5 fusion.119
  250.8 2.6 fusion.118
  285.5 4.4 fusion.28
  300.8 3.6 fusion.26
  306.7 2.0 fusion.55
  311.3 3.5 convolution_convert_fusion
  322.6 2.2 convolution_convert_fusion.4
  326.5 2.2 convolution_convert_fusion.1
  330.7 2.4 convert_reduce_fusion.6
  342.4 2.4 fusion.37
  353.5 5.2 fusion.39
  358.9 2.3 stack.112
  362.6 165.0 %shard_map.213 = (bf16[28,96,768]{2,1,0:T(8,128)(2,1)}, f32[32,128]{1,0:T(8,128)}) custom-call(bf16[3072,384]{1,0:T(8,128)(2,1)} %get-tuple-element.49.refs_0_, bf16[768,384]{1,0:T(8,128)(2,1)} %get-tuple-element.50.refs_1_, bf16[768,384]{1,0:T(8,128)(2,1)} %get-tuple-element.51.refs_2_, bf16[768,384]{1,0:T(8,128)(2,1)} %get-tuple-element.52.refs_3_, ...), custom_call_target="tpu_custom_call" | custom-call | tf_op jit(solution)/shard_map/pallas_call | solution.py:1030
  (235 shorter events, 152.8 us)
Async XLA Ops:
  168.4 13.1 %copy-start.1 = (f32[3,384,768]{2,1,0:T(8,128)S(1)}, f32[3,384,768]{2,1,0:T(8,128)}, u32[]{:S(2)}) copy-start(f32[3,384,768]{2,1,0:T(8,128)} %get-tuple-element.37) | copy-start | bytes 10616836
  188.3 5.9 %copy-start.12 = (bf16[384,768]{1,0:T(8,128)(2,1)S(1)}, bf16[384,768]{1,0:T(8,128)(2,1)}, u32[]{:S(2)}) copy-start(bf16[384,768]{1,0:T(8,128)(2,1)} %copy-done.11) | copy-start | bytes 1769476
  188.3 5.9 %copy-start.54 = (bf16[384,3072]{1,0:T(8,128)(2,1)S(1)}, bf16[384,3072]{1,0:T(8,128)(2,1)}, u32[]{:S(2)}) copy-start(bf16[384,3072]{1,0:T(8,128)(2,1)} %get-tuple-element.39) | copy-start | bytes 7077892
  203.2 4.4 copy-start.32
  207.6 3.9 copy-start.7
  207.6 3.9 copy-start.18
  212.6 6.1 %copy-start.43 = (f32[768]{0:T(1024)S(1)}, f32[768]{0:T(1024)}, u32[]{:S(2)}) copy-start(f32[768]{0:T(1024)} %get-tuple-element.82) | copy-start | bytes 9220
  285.4 4.5 copy-start.2
  285.4 4.5 copy-start.23
  285.4 4.5 copy-start.33
  300.7 3.6 copy-start.19
  300.7 3.6 copy-start.20
  300.7 3.6 copy-start.21
  300.7 3.7 copy-start.24
  300.7 3.7 copy-start.25
  300.8 3.7 copy-start.26
  306.7 4.6 copy-start.48
  310.1 20.6 %copy-start.50 = (f32[384]{0:T(512)}, f32[384]{0:T(512)S(1)}, u32[]{:S(2)}) copy-start(f32[384]{0:T(512)S(1)} %broadcast_multiply_fusion) | copy-start | bytes 4612
  353.4 5.3 copy-start.8
  353.4 5.4 copy-start.45
  353.4 5.4 copy-start.46
  353.5 5.4 copy-start.47
  362.6 169.8 %copy-start.34 = (f32[384,768]{1,0:T(8,128)S(1)}, f32[384,768]{1,0:T(8,128)}, u32[]{:S(2)}) copy-start(f32[384,768]{1,0:T(8,128)} %fusion.39) | copy-start | bytes 3538948
  533.2 3.5 copy-start
  (31 other events, 52.4 us)
